TPU v7x, 32 devices: a whole 2x2x4 slice. The times are simulated.
32 devices in a mesh: cluster: 8 (over y, x, core), batch: 4 (over z).
Axes of the slice: x: 2, y: 2, z: 4, core: 2. Of those that a mesh axis runs over, the one named last changes fastest.
Arguments:
- features: bfloat16 [4, 8192, 128], P('batch', 'cluster'), may hold values from -6 to 6
- tiles: bfloat16 [4, 64, 5, 128, 128], P('batch', 'cluster'), may hold values from 0 to 1
- columns: int32 [4, 64, 5], P('batch', 'cluster'), may hold values from 0 to 63, as said below
- live_blocks: int32 [4, 64], P('batch', 'cluster'), may hold values from 1 to 5, as said below
- edge_counts: int32 [4, 64, 5, 128], P('batch', 'cluster'), may hold values from 1 to 8
- weight: bfloat16 [256, 128], replicated, may hold values from -0.375 to 0.375
- bias: float32 [128], replicated, may hold values from -3 to 3
- cotangent: bfloat16 [4, 8192, 128], P('batch', 'cluster'), may hold values from -6 to 6
Outputs:
- output: bfloat16 [4, 8192, 128], P('batch', 'cluster')
- grad_features: float32 [4, 8192, 128], P('batch', 'cluster')
- grad_weight: float32 [256, 128], replicated
- grad_bias: float32 [128], replicated
Inputs may be any that keep to these rules, and one draw needn't show every extreme that they name: columns[c, p, s] lies within 2 panels of p. Inside a cluster the slots of a row panel that fall inside the cluster name distinct panels; slots that would fall outside the cluster name p itself. The first live_blocks[c, p] slots of row panel p are its nonzero blocks; the others are padding.
All inputs are finite; a program needn't handle non-finite values.
Results may differ from a plain program's by a relative error of at most 0.006.
Values may be sent and summed in bfloat16 or wider, within the bound.
No kernel may reach another device: no remote copies, remote signals or barrier semaphores. Data moves between devices by JAX's collectives and lax.ppermute only.
A program may use at most 64 MiB of HBM per device.

v0:
```python
import math

import jax
import jax.numpy as jnp
from jax import lax
from jax.sharding import PartitionSpec as P

REACH = 2


def shifted(block, axis, distance):
    devices = range(lax.axis_size(axis))
    route = [(i - distance, i) for i in devices if i - distance in devices]
    return lax.ppermute(block, axis, route)


def extended_2(block, sides, width):
    for axis, dim in sides:
        count = lax.axis_size(axis)
        forward = [(i, i + 1) for i in range(count - 1)]
        backward = [(target, source) for source, target in forward]
        low = lax.ppermute(
            lax.slice_in_dim(block, block.shape[dim] - width, None, axis=dim), axis, forward
        )
        high = lax.ppermute(lax.slice_in_dim(block, 0, width, axis=dim), axis, backward)
        block = jnp.concatenate([low, block, high], axis=dim)
    return block


def silu_slope(values):
    sigmoid_v = jax.nn.sigmoid(values)
    return sigmoid_v * (1.0 + values * (1.0 - sigmoid_v))


def pass_along(terms, offset):
    return shifted(terms.astype(jnp.bfloat16), "cluster", offset).astype(terms.dtype)


def body(features, tiles, columns, live_blocks, edge_counts, weight, bias, cotangent):
    nodes_dev = features.shape[1]
    width = features.shape[2]
    panels_dev = tiles.shape[1]
    slots = tiles.shape[2]
    block = tiles.shape[3]
    span_panels = panels_dev + 2 * REACH
    first_panel = lax.axis_index("cluster") * panels_dev
    live_mask = lax.broadcasted_iota(jnp.int32, (panels_dev, slots), 1) < live_blocks[0][:, None]
    position = columns[0] - first_panel + REACH
    slot_grid = lax.broadcasted_iota(jnp.int32, (panels_dev, slots, span_panels), 2)
    onehot = jnp.where(live_mask[:, :, None] & (position[:, :, None] == slot_grid), 1.0, 0.0)
    onehot_flat = onehot.reshape(panels_dev * slots, span_panels)
    degree = jnp.sum(jnp.where(live_mask[:, :, None], edge_counts[0], 0), axis=1).astype(
        jnp.float32
    )
    extended = extended_2(features, (("cluster", 1),), REACH * block)
    ext_panels = extended[0].reshape(span_panels, block * width)
    picked = jnp.dot(
        onehot_flat.astype(jnp.bfloat16), ext_panels, preferred_element_type=jnp.float32
    )
    picked = picked.astype(jnp.bfloat16).reshape(panels_dev, slots, block, width)
    summed = jnp.einsum("psrc,pscf->prf", tiles[0], picked, preferred_element_type=jnp.float32)
    neighbor_mean = (summed / degree[:, :, None]).astype(jnp.bfloat16).reshape(nodes_dev, width)
    node_feats = features[0]
    pre_act = jnp.dot(node_feats, weight[:width], preferred_element_type=jnp.float32)
    pre_act = (
        pre_act + jnp.dot(neighbor_mean, weight[width:], preferred_element_type=jnp.float32) + bias
    )
    output = jax.nn.silu(pre_act).astype(jnp.bfloat16)
    slope_bf = (cotangent[0].astype(jnp.float32) * silu_slope(pre_act)).astype(jnp.bfloat16)
    joined = jnp.concatenate([node_feats, neighbor_mean], axis=1)
    weight_term = lax.dot_general(
        joined, slope_bf, (((0,), (0,)), ((), ())), preferred_element_type=jnp.float32
    )
    bias_term = jnp.sum(slope_bf.astype(jnp.float32), axis=0)
    scaled = lax.dot_general(
        slope_bf, weight[width:], (((1,), (1,)), ((), ())), preferred_element_type=jnp.float32
    )
    scaled = (scaled / degree.reshape(nodes_dev)[:, None]).astype(jnp.bfloat16)
    contrib = jnp.einsum(
        "psrc,prf->pscf",
        tiles[0],
        scaled.reshape(panels_dev, block, width),
        preferred_element_type=jnp.float32,
    )
    placed = lax.dot_general(
        onehot_flat,
        contrib.reshape(panels_dev * slots, block * width),
        (((0,), (0,)), ((), ())),
        precision=lax.Precision.HIGHEST,
        preferred_element_type=jnp.float32,
    )
    placed = placed.reshape(span_panels, block, width)
    lower_terms = placed[:REACH]
    upper_terms = placed[REACH + panels_dev :]
    own_terms = placed[REACH : REACH + panels_dev]
    from_lower = pass_along(upper_terms, 1)
    from_upper = pass_along(lower_terms, -1)
    own_terms = own_terms.at[:REACH].add(from_lower)
    own_terms = own_terms.at[panels_dev - REACH :].add(from_upper)
    grad_features = lax.dot_general(
        slope_bf, weight[:width], (((1,), (1,)), ((), ())), preferred_element_type=jnp.float32
    )
    grad_features = grad_features + own_terms.reshape(nodes_dev, width)
    grad_scale = 1.0 / math.sqrt(lax.axis_size("batch") * lax.axis_size("cluster") * nodes_dev)
    weight_total, bias_total = lax.psum((weight_term, bias_term), ("cluster", "batch"))
    return (output[None], grad_features[None], weight_total * grad_scale, bias_total * grad_scale)


def solution(mesh):
    in_specs = (
        P("batch", "cluster", None),
        P("batch", "cluster", None, None, None),
        P("batch", "cluster", None),
        P("batch", "cluster"),
        P("batch", "cluster", None, None),
        P(),
        P(),
        P("batch", "cluster", None),
    )
    out_specs = (P("batch", "cluster", None), P("batch", "cluster", None), P(), P())
    return jax.shard_map(body, mesh=mesh, in_specs=in_specs, out_specs=out_specs, check_vma=False)
```

profile of v0, /device:TPU:0, one launch (start us, length us, event | category | flops | bytes accessed | tf_op | source)
XLA Modules:
  0.0 207.7 jit_solution(6483964147516793268)
XLA Ops:
  7.2 0.0 copy-start
  7.2 0.0 copy-start.1
  7.2 0.0 all-reduce.2.cloned.1.call-start
  7.2 1.0 fusion.44
  8.2 2.4 %collective-permute-start = (bf16[1,256,128]{2,1,0:T(8,128)(2,1)S(1)}, bf16[1,256,128]{2,1,0:T(8,128)(2,1)S(1)}, u32[]{:S(2)}, u32[]{:S(2)}) collective-permute-start(bf16[1,256,128]{2,1,0:T(8,128)(2,1)S(1)} %get-tuple-element.33), channel_id=1, source_target_pairs={{0,4},{4,8},{8,12},{12,16},{16,20},{20,24},{24,28},{1,5},{5,9},{9,... | collective-permute-start | bytes 196616 | tf_op jit(solution)/shard_map/ppermute | solution.py:22
  10.6 1.3 collective-permute-start.1
  11.9 0.7 iota_compare_fusion.1
  12.6 0.1 copy.16
  12.7 0.8 fusion.39
  13.5 0.8 copy.17
  14.2 1.2 fusion.32
  15.4 0.1 fusion.27
  15.6 0.0 collective-permute-done
  15.6 0.3 collective-permute-done.1
  15.9 0.0 copy-done.1
  15.9 0.3 reshape_squeeze.3
  16.2 0.5 fusion.3
  16.6 0.3 copy.25
  17.0 0.0 copy-done
  17.0 0.0 copy-start.2
  17.0 0.0 copy-start.3
  17.0 0.0 copy-start.4
  17.0 0.5 fusion.15
  17.5 0.0 copy-start.5
  17.5 0.3 copy-done.2
  17.8 0.1 copy-done.3
  18.0 0.0 copy-done.4
  18.0 1.1 convert_reduce_fusion
  19.1 0.0 copy-done.5
  19.1 0.2 fusion.11
  19.4 2.1 convolution_bitcast_fusion
  21.4 3.2 %copy.19 = f32[8,5,128,128]{3,2,1,0:T(8,128)} copy(f32[8,5,128,128]{2,3,1,0:T(8,128)} %convolution_bitcast_fusion) | data formatting | bytes 5242880 | tf_op jit(solution)/shard_map/psrc,prf->pscf/dot_general | solution.py:79
  24.7 4.6 %fusion.45 = (bf16[12,16384]{1,0:T(8,128)(2,1)S(1)}, f32[12,16384]{1,0:T(8,128)S(1)}) fusion(f32[40,12]{1,0:T(8,128)S(1)} %select_n.27, f32[5,8,128,128]{3,2,1,0:T(8,128)} %bitcast.90), kind=kOutput, calls=%fused_computation.59 | convolution fusion | flops 94568448 | bytes 3803008 | tf_op jit(solution)/shard_map/dot_general | solution.py:85
  29.2 0.0 copy-start.6
  29.2 0.1 slice_bitcast_fusion.1
  29.3 0.1 slice_bitcast_fusion
  29.4 0.8 copy-done.6
  30.2 1.0 fusion.18
  31.2 43.6 %psum.15 = f32[128]{0:T(128)S(1)} all-reduce(f32[128]{0:T(128)S(1)} %get-tuple-element.28), channel_id=1, replica_groups=mesh['cluster'=8,'batch'=4] {'cluster','batch'}, use_global_device_ids=true, to_apply=%region_3.4 | all-reduce | flops 128 | bytes 1024 | tf_op jit(solution)/shard_map/psum | solution.py:105
  74.8 0.0 all-reduce.2.cloned.1.call-update
  74.8 0.1 slice_bitcast_fusion.2
  74.9 0.5 broadcast_multiply_fusion.1
  75.4 1.3 collective-permute-start.2
  76.7 1.3 collective-permute-start.3
  78.0 0.1 copy.20
  78.2 120.0 %all-reduce.2.cloned.1.call-done = f32[256,128]{1,0:T(8,128)} async-done(((f32[256,128]{1,0:T(8,128)}), f32[256,128]{1,0:T(8,128)}) %all-reduce.2.cloned.1.call-update) | async-done | bytes 131088 | tf_op jit(solution)/shard_map/psum | solution.py:105
  198.2 1.6 broadcast_multiply_fusion
  199.7 0.0 collective-permute-done.2
  199.7 0.0 collective-permute-done.3
  199.8 1.0 fusion.36
  (9 shorter events, 0.1 us)
Async XLA Ops:
  7.2 9.8 %copy-start = (bf16[1,8,5,128,128]{4,3,2,1,0:T(8,128)(2,1)S(1)}, bf16[1,8,5,128,128]{4,3,2,1,0:T(8,128)(2,1)}, u32[]{:S(2)}) copy-start(bf16[1,8,5,128,128]{4,3,2,1,0:T(8,128)(2,1)} %param.13) | copy-start | bytes 3932164
  7.2 8.7 %copy-start.1 = (bf16[1,1024,128]{2,1,0:T(8,128)(2,1)S(1)}, bf16[1,1024,128]{2,1,0:T(8,128)(2,1)}, u32[]{:S(2)}) copy-start(bf16[1,1024,128]{2,1,0:T(8,128)(2,1)} %param.12) | copy-start | bytes 786436
  7.2 191.0 %all-reduce.2.cloned.1.call-start = ((), (), s32[]{:S(2)}) async-start(), calls=%async_computation | async-start | bytes 262144 | tf_op jit(solution)/shard_map/psum | solution.py:105
  8.2 7.3 %collective-permute-start = (bf16[1,256,128]{2,1,0:T(8,128)(2,1)S(1)}, bf16[1,256,128]{2,1,0:T(8,128)(2,1)S(1)}, u32[]{:S(2)}, u32[]{:S(2)}) collective-permute-start(bf16[1,256,128]{2,1,0:T(8,128)(2,1)S(1)} %get-tuple-element.33), channel_id=1, source_target_pairs={{0,4},{4,8},{8,12},{12,16},{16,20},{20,24},{24,28},{1,5},{5,9},{9,... | collective-permute-start | bytes 196616 | tf_op jit(solution)/shard_map/ppermute | solution.py:22
  10.6 5.3 %collective-permute-start.1 = (bf16[1,256,128]{2,1,0:T(8,128)(2,1)S(1)}, bf16[1,256,128]{2,1,0:T(8,128)(2,1)S(1)}, u32[]{:S(2)}, u32[]{:S(2)}) collective-permute-start(bf16[1,256,128]{2,1,0:T(8,128)(2,1)S(1)} %get-tuple-element.34), channel_id=1, source_target_pairs={{4,0},{8,4},{12,8},{16,12},{20,16},{24,20},{28,24},{5,1},{9,5},{13... | collective-permute-start | bytes 196616 | tf_op jit(solution)/shard_map/ppermute | solution.py:25
  17.0 0.8 copy-start.2
  17.0 1.0 copy-start.3
  17.0 1.0 copy-start.4
  17.5 1.6 copy-start.5
  29.2 1.0 copy-start.6
  75.4 124.3 %collective-permute-start.2 = (bf16[2,128,128]{2,1,0:T(8,128)(2,1)S(1)}, bf16[2,128,128]{2,1,0:T(8,128)(2,1)S(1)}, u32[]{:S(2)}, u32[]{:S(2)}) collective-permute-start(bf16[2,128,128]{2,1,0:T(8,128)(2,1)S(1)} %bitcast.95), channel_id=1, source_target_pairs={{0,4},{4,8},{8,12},{12,16},{16,20},{20,24},{24,28},{1,5},{5,9},{9,... | collective-permute-start | bytes 196616 | tf_op jit(solution)/shard_map/ppermute | solution.py:14
  76.7 123.0 %collective-permute-start.3 = (bf16[2,128,128]{2,1,0:T(8,128)(2,1)S(1)}, bf16[2,128,128]{2,1,0:T(8,128)(2,1)S(1)}, u32[]{:S(2)}, u32[]{:S(2)}) collective-permute-start(bf16[2,128,128]{2,1,0:T(8,128)(2,1)S(1)} %bitcast.94), channel_id=1, source_target_pairs={{4,0},{8,4},{12,8},{16,12},{20,16},{24,20},{28,24},{5,1},{9,5},{13... | collective-permute-start | bytes 196616 | tf_op jit(solution)/shard_map/ppermute | solution.py:14
Sparse Core Ops, SparseCore 0:
  74.9 123.1 all-reduce.1
where the time goes:
time: 208 us
  waiting for transfers between devices  120 us (58%)
  blocking collectives  43.6 us (21%)
  between operations  14.3 us (7%)
  matrix products  12.2 us (6%)
  local copies, waits for them, and re-layouts  7.32 us (4%)
  starting transfers between devices  6.27 us (3%)
  other arithmetic  3.71 us (2%)
    psum x1, waiting for transfers between devices, body(): lax.psum((weight_term, bias_term), ('cluster', 'batch'))  120 us
    psum x1, blocking collectives, body(): lax.psum((weight_term, bias_term), ('cluster', 'batch'))  43.6 us
    dot_general x1, matrix products, body(): lax.dot_general(onehot_flat, contrib.reshape(panels_dev * slots, block *...  4.57 us
  transfers between devices with their start and end apart: 5, of which 2 were waited for; matrix products, arithmetic and copies ran while one was open for 3% of the time, Pallas kernels for 0%

commit v1 on v0

v1 whole, which is shorter than its diff:
```python
import functools
import math

import jax
import jax.numpy as jnp
from jax import lax
from jax.experimental import pallas as pl
from jax.experimental.pallas import tpu as pltpu
from jax.sharding import PartitionSpec as P

REACH = 2
TAIL = 16
F32 = jnp.float32
BF16 = jnp.bfloat16
VMEM = pl.BlockSpec(memory_space=pltpu.VMEM)
SMEM = pl.BlockSpec(memory_space=pltpu.SMEM)


def dot(a, b):
    return jnp.dot(a, b, preferred_element_type=F32)


def place():
    return lax.axis_index("cluster"), lax.axis_index("batch")


def half_of(clusters, batches):
    c, b = place()
    total = jnp.int32(0)
    for index, size in ((c, clusters), (b, batches)):
        for bit in range((size - 1).bit_length()):
            total = total + ((index >> bit) & 1)
    return total % 2


def activation(pre):
    sig = 1.0 / (1.0 + jnp.exp(-pre))
    return pre * sig, sig * (1.0 + pre * (1.0 - sig))


def split3(value):
    first = value.astype(BF16)
    rest = value - first.astype(F32)
    second = rest.astype(BF16)
    third = (rest - second.astype(F32)).astype(BF16)
    return first, second, third


def tail_rows(total):
    first, second, third = split3(jnp.broadcast_to(total, (TAIL, total.shape[1])))
    row = lax.broadcasted_iota(jnp.int32, first.shape, 0)
    zero = jnp.zeros_like(first)
    return jnp.where(row == 0, first, jnp.where(row == 1, second, jnp.where(row == 2, third, zero)))


def tail_total(rows):
    return jnp.sum(rows.astype(F32), axis=0, keepdims=True)


def edges(panels):
    par = lax.axis_index("cluster") % 2
    return (panels - REACH) * (1 - par), (panels - REACH) * par, par


def band(cols, live, tiles, base, outside, first):
    slots = tiles.shape[2]
    rows = []
    for j in range(REACH):
        p = base + j
        blocks = []
        for m in range(REACH):
            found = jnp.int32(0)
            for s in range(slots):
                hit = (s < live[0, p]) & (cols[0, p, s] - first == outside + m)
                found = found + jnp.where(hit, s + 1, 0)
            tile = tiles[0, p, jnp.maximum(found - 1, 0)]
            blocks.append(jnp.where(found > 0, tile, jnp.zeros_like(tile)))
        rows.append(jnp.concatenate(blocks, axis=1))
    return jnp.concatenate(rows, axis=0)


def own_slot(cols, live, p, s, first, panels):
    q = cols[0, p, s] - first
    return jnp.where((s < live[0, p]) & (q >= 0) & (q < panels), q, panels)


def forward_near(
    cols, live, feat, mate, tiles, counts, weight, bias, cot,
    out_near, slope_t, recip, t_far, s_far, r_far, p_far, c_far, f_far, w_part, b_part, mate_ret,
    own,
):
    panels, slots, block = tiles.shape[1], tiles.shape[2], tiles.shape[3]
    width = feat.shape[2]
    first = lax.axis_index("cluster") * panels
    edge, far, par = edges(panels)
    mid = panels - 2 * REACH
    order = [REACH + j for j in range(mid)] + [edge + j for j in range(REACH)] + [far + j for j in range(REACH)]
    near = (mid + REACH) * block
    span = REACH * block
    own[0 : panels * block, :] = feat[0]
    own[panels * block :, :] = jnp.zeros((block, width), BF16)
    rows = []
    for p in order:
        count = counts[0, p]
        slot = lax.broadcasted_iota(jnp.int32, count.shape, 0)
        kept = jnp.where(slot < live[0, p], count, 0).astype(F32)
        rows.append(jnp.sum(kept, axis=0, keepdims=True))
    recip_rows = 1.0 / jnp.concatenate(rows, axis=0)
    recip[...] = recip_rows
    recip_cols = recip_rows.T

    def own_sum(p):
        lhs = jnp.concatenate([tiles[0, p, s] for s in range(slots)], axis=1)
        rhs = []
        for s in range(slots):
            q = own_slot(cols, live, p, s, first, panels)
            rhs.append(own[pl.ds(pl.multiple_of(q * block, block), block), :])
        return dot(lhs, jnp.concatenate(rhs, axis=0))

    sums = [own_sum(p) for p in order]
    t_mate = band(cols, live, tiles, edge, panels - (panels + REACH) * par, first)
    across = dot(t_mate, mate[...])
    for j in range(REACH):
        sums[mid + j] = sums[mid + j] + across[j * block : (j + 1) * block]
    means = [(sums[j] * recip_cols[:, j : j + 1]).astype(BF16) for j in range(mid + REACH)]
    edge_rows = pl.ds(pl.multiple_of(edge * block, block), span)
    far_rows = pl.ds(pl.multiple_of(far * block, block), span)
    mid_rows = slice(REACH * block, REACH * block + mid * block)
    mean = jnp.concatenate(means, axis=0)
    node = jnp.concatenate([feat[0, mid_rows, :], feat[0, edge_rows, :]], axis=0)
    cot_near = jnp.concatenate([cot[0, mid_rows, :], cot[0, edge_rows, :]], axis=0)
    joined = jnp.concatenate([node, mean], axis=1)
    pre = dot(joined, weight[...]) + bias[...]
    act, rise = activation(pre)
    out_near[...] = act.astype(BF16)
    slope = (cot_near.astype(F32) * rise).astype(BF16)
    turned = slope.T
    slope_t[...] = turned
    w_part[...] = dot(turned, joined)
    b_part[...] = jnp.broadcast_to(jnp.sum(slope.astype(F32), axis=0, keepdims=True), b_part.shape)
    scale_row = jnp.concatenate([recip_rows[mid + j : mid + j + 1] for j in range(REACH)], axis=1)
    scaled = (dot(weight[width:, :], turned[:, mid * block :]) * scale_row).astype(BF16)
    back = dot(scaled, t_mate).astype(BF16)
    for m in range(REACH):
        mate_ret[m * block : (m + 1) * block, :] = back[:, m * block : (m + 1) * block]
    t_far[...] = band(cols, live, tiles, far, (panels + REACH) * par - REACH, first)
    for j in range(REACH):
        here = slice(j * block, (j + 1) * block)
        s_far[here, :] = sums[mid + REACH + j]
        col = recip_cols[:, mid + REACH + j : mid + REACH + j + 1]
        r_far[here, :] = jnp.broadcast_to(col, (block, width))
    f_far[...] = feat[0, far_rows, :]
    c_far[...] = cot[0, far_rows, :]
    p_far[...] = dot(feat[0, far_rows, :], weight[:width, :]) + bias[...]


def forward_far(
    halo, t_far, s_far, r_far, p_far, c_far, f_far, weight, w_part, b_part, mate_ret,
    out_far, slope_t, kept, send,
    *, clusters, batches,
):
    width = f_far.shape[1]
    half = half_of(clusters, batches)
    mean = ((s_far[...] + dot(t_far[...], halo[...])) * r_far[...]).astype(BF16)
    pre = p_far[...] + dot(mean, weight[width:, :])
    act, rise = activation(pre)
    out_far[...] = act.astype(BF16)
    slope = (c_far[...].astype(F32) * rise).astype(BF16)
    turned = slope.T
    slope_t[...] = turned
    total = w_part[...] + dot(turned, jnp.concatenate([f_far[...], mean], axis=1))
    b_total = b_part[0:1, :] + jnp.sum(slope.astype(F32), axis=0, keepdims=True)
    low, high = total[:, :width], total[:, width:]
    rows = low.shape[0]
    kept[0:rows, :] = jnp.where(half == 0, low, high)
    kept[rows:, :] = jnp.broadcast_to(b_total, (kept.shape[0] - rows, width))
    send[0:rows, :] = jnp.where(half == 0, high, low).astype(BF16)
    send[rows : rows + TAIL, :] = tail_rows(b_total)
    send[rows + TAIL :, :] = mate_ret[...]


def return_far(weight, slope_t, t_far, recip, far_ret):
    width = weight.shape[1]
    panels, block = recip.shape
    scale_row = jnp.concatenate([recip[panels - REACH + j : panels - REACH + j + 1, :] for j in range(REACH)], axis=1)
    scaled = (dot(weight[width:, :], slope_t[...]) * scale_row).astype(BF16)
    back = dot(scaled, t_far[...]).astype(BF16)
    for m in range(REACH):
        far_ret[m * block : (m + 1) * block, :] = back[:, m * block : (m + 1) * block]


def first_sum(kept, got, total):
    rows = kept.shape[0] - TAIL
    total[0:rows, :] = (kept[0:rows, :] + got[0:rows, :].astype(F32)).astype(BF16)
    total[rows:, :] = tail_rows(kept[rows : rows + 1, :] + tail_total(got[rows : rows + TAIL, :]))


def next_sum(mine, got, total):
    rows = mine.shape[0] - TAIL
    total[0:rows, :] = (mine[0:rows, :].astype(F32) + got[0:rows, :].astype(F32)).astype(total.dtype)
    b_total = tail_total(mine[rows:, :]) + tail_total(got[rows:, :])
    if total.dtype == BF16:
        total[rows:, :] = tail_rows(b_total)
    else:
        total[rows:, :] = jnp.broadcast_to(b_total, (TAIL, b_total.shape[1]))


def finish(mine, got, grad, grad_bias, *, clusters, batches, scale):
    half = half_of(clusters, batches)
    rows = got.shape[0]
    own = mine[0:rows, :].T * scale
    other = got[...].T * scale
    grad[0:rows, :] = jnp.where(half == 0, own, other)
    grad[rows:, :] = jnp.where(half == 0, other, own)
    grad_bias[...] = mine[rows : rows + 1, :] * scale


def backward(cols, live, tiles, weight, near_t, far_t, recip, total):
    panels, slots, block = tiles.shape[1], tiles.shape[2], tiles.shape[3]
    width = weight.shape[1]
    first = lax.axis_index("cluster") * panels
    edge, far, _ = edges(panels)
    mid = panels - 2 * REACH
    order = [REACH + j for j in range(mid)] + [edge + j for j in range(REACH)] + [far + j for j in range(REACH)]
    near = mid + REACH
    parts = [near_t[:, j * block : (j + 1) * block] for j in range(near)]
    parts += [far_t[:, j * block : (j + 1) * block] for j in range(REACH)]
    for j, p in enumerate(order):
        total[p] = dot(weight[:width, :], parts[j])
    total[panels] = jnp.zeros((width, block), F32)
    for j, p in enumerate(order):
        scaled = (dot(weight[width:, :], parts[j]) * recip[j : j + 1, :]).astype(BF16)
        spread = dot(scaled, jnp.concatenate([tiles[0, p, s] for s in range(slots)], axis=1))
        for s in range(slots):
            q = own_slot(cols, live, p, s, first, panels)
            total[q] = total[q] + spread[:, s * block : (s + 1) * block]


def gather_outputs(total, from_mate, from_far, out_near, out_far, grad, output):
    panels, block = total.shape[0] - 1, total.shape[2]
    edge, far, _ = edges(panels)
    mid = panels - 2 * REACH
    skip = from_mate.shape[0] - REACH * block
    for j in range(mid):
        p = REACH + j
        grad[0, p * block : (p + 1) * block, :] = total[p].T
    for base, source, start in ((edge, from_mate, skip), (far, from_far, 0)):
        for j in range(REACH):
            term = source[start + j * block : start + (j + 1) * block, :].astype(F32)
            rows = pl.ds(pl.multiple_of((base + j) * block, block), block)
            grad[0, rows, :] = (total[base + j] + term).T
    output[0, REACH * block : (REACH + mid) * block, :] = out_near[0 : mid * block, :]
    output[0, pl.ds(pl.multiple_of(edge * block, block), REACH * block), :] = out_near[mid * block :, :]
    output[0, pl.ds(pl.multiple_of(far * block, block), REACH * block), :] = out_far[...]


def call(kernel, name, shapes, specs, scratch=(), flops=0, nbytes=0, **static):
    single = not isinstance(shapes, (list, tuple))
    body = functools.partial(kernel, **static) if static else kernel
    return pl.pallas_call(
        body,
        out_shape=shapes,
        in_specs=specs,
        out_specs=VMEM if single else [VMEM] * len(shapes),
        scratch_shapes=list(scratch),
        compiler_params=pltpu.CompilerParams(vmem_limit_bytes=24 << 20),
        cost_estimate=pl.CostEstimate(flops=flops, bytes_accessed=nbytes, transcendentals=0),
        name=name,
    )


def swap(block, c_flip, b_flip):
    nc, nb = lax.axis_size("cluster"), lax.axis_size("batch")
    if b_flip == 0:
        return lax.ppermute(block, "cluster", [(c, c ^ c_flip) for c in range(nc)])
    pairs = [(c * nb + b, (c ^ c_flip) * nb + (b ^ b_flip)) for c in range(nc) for b in range(nb)]
    return lax.ppermute(block, ("cluster", "batch"), pairs)


def swap_far(block):
    n = lax.axis_size("cluster")
    return lax.ppermute(block, "cluster", [(c, (c + 1) % n if c % 2 else (c - 1) % n) for c in range(n)])


def body(features, tiles, columns, live_blocks, edge_counts, weight, bias, cotangent):
    nodes, width = features.shape[1], features.shape[2]
    panels, slots, block = tiles.shape[1], tiles.shape[2], tiles.shape[3]
    hidden = weight.shape[1]
    nc, nb = lax.axis_size("cluster"), lax.axis_size("batch")
    span = REACH * block
    near = nodes - span
    shape = jax.ShapeDtypeStruct
    par = lax.axis_index("cluster") % 2
    low, high = features[0, :span], features[0, nodes - span :]
    far_halo = swap_far(jnp.where(par == 0, low, high))
    mate_halo = swap(jnp.where(par == 0, high, low), 1, 0)
    bias_row = bias.reshape(1, hidden)
    sizes = dict(clusters=nc, batches=nb)
    (out_near, near_t, recip, t_far, s_far, r_far, p_far, c_far, f_far, w_part, b_part, mate_ret) = call(
        forward_near,
        "forward_near",
        [
            shape((near, hidden), BF16),
            shape((hidden, near), BF16),
            shape((panels, block), F32),
            shape((span, span), BF16),
            shape((span, width), F32),
            shape((span, width), F32),
            shape((span, hidden), F32),
            shape((span, hidden), BF16),
            shape((span, width), BF16),
            shape((hidden, 2 * width), F32),
            shape((8, hidden), F32),
            shape((span, block), BF16),
        ],
        [SMEM, SMEM] + [VMEM] * 7,
        [pltpu.VMEM((nodes + block, width), BF16)],
        flops=4 * 10**8,
        nbytes=4 << 20,
    )(columns, live_blocks, features, mate_halo, tiles, edge_counts, weight, bias_row, cotangent)
    rows = hidden + TAIL
    out_far, far_t, kept, send = call(
        forward_far,
        "forward_far",
        [
            shape((span, hidden), BF16),
            shape((hidden, span), BF16),
            shape((rows, width), F32),
            shape((rows + span, width), BF16),
        ],
        [VMEM] * 11,
        flops=10**8,
        nbytes=1 << 20,
        **sizes,
    )(far_halo, t_far, s_far, r_far, p_far, c_far, f_far, weight, w_part, b_part, mate_ret)
    got = swap(send, 1, 0)
    far_ret = call(return_far, "return_far", shape((span, block), BF16), [VMEM] * 4, flops=10**7, nbytes=1 << 18)(
        weight, far_t, t_far, recip
    )
    from_far = swap_far(far_ret)
    total = call(backward, "backward", shape((panels + 1, width, block), F32), [SMEM] * 2 + [VMEM] * 5, flops=4 * 10**8, nbytes=3 << 20)(
        columns, live_blocks, tiles, weight, near_t, far_t, recip
    )
    mine = call(first_sum, "first_sum", shape((rows, width), BF16), [VMEM] * 2, flops=10**5, nbytes=10**5)(kept, got)
    steps = [((1 << i) | 1, 0) for i in range(1, (nc - 1).bit_length())]
    steps += [(1, 1 << i) for i in range((nb - 1).bit_length())]
    for i, (c_flip, b_flip) in enumerate(steps):
        other = swap(mine, c_flip, b_flip)
        kind = F32 if i == len(steps) - 1 else BF16
        mine = call(next_sum, "next_sum", shape((rows, width), kind), [VMEM] * 2, flops=10**5, nbytes=10**5)(mine, other)
    last = swap(mine[:hidden], 1, 0)
    scale = 1.0 / math.sqrt(nb * nc * nodes)
    grad_weight, grad_bias = call(
        finish, "finish", [shape((2 * width, hidden), F32), shape((1, hidden), F32)], [VMEM] * 2, flops=10**5, nbytes=10**5, scale=scale, **sizes
    )(mine, last)
    grad_features, output = call(
        gather_outputs,
        "gather_outputs",
        [shape((1, nodes, width), F32), shape((1, nodes, hidden), BF16)],
        [VMEM] * 5,
        flops=10**6,
        nbytes=2 << 20,
    )(total, got, from_far, out_near, out_far)
    return output, grad_features, grad_weight, grad_bias.reshape(hidden)


def solution(mesh):
    in_specs = (
        P("batch", "cluster", None),
        P("batch", "cluster", None, None, None),
        P("batch", "cluster", None),
        P("batch", "cluster"),
        P("batch", "cluster", None, None),
        P(),
        P(),
        P("batch", "cluster", None),
    )
    out_specs = (P("batch", "cluster", None), P("batch", "cluster", None), P(), P())
    return jax.shard_map(body, mesh=mesh, in_specs=in_specs, out_specs=out_specs, check_vma=False)
```

time: 208 us -> 36.8 us (0.18)
  waiting for transfers between devices: 120 us -> 11.7 us
  blocking collectives: 43.6 us -> 0 us
  between operations: 14.3 us -> 0.75 us
  matrix products: 12.2 us -> 0 us
  Pallas kernels: 0 us -> 6.81 us
  starting transfers between devices: 6.27 us -> 9.35 us
  other arithmetic: 3.71 us -> 0.89 us
    psum x1 -> x0, waiting for transfers between devices: 120 us -> none  [body(): lax.psum((weight_term, bias_term), ('cluster', 'batch'))]
    psum x1 -> x0, blocking collectives: 43.6 us -> none  [body(): lax.psum((weight_term, bias_term), ('cluster', 'batch'))]
    dot_general x9 -> x0, matrix products: 12.2 us -> none  [the longest x1 4.57 us: body(): lax.dot_general(onehot_flat, contrib.reshape(panels_dev * slots, block *...]
    ppermute x4 -> x9, waiting for transfers between devices: 0.3 us -> 11.7 us  [the longest x5 7.7 us: swap(): return lax.ppermute(block, 'cluster', [(c, c ^ c_flip) for c in range(nc)])]
    pallas_call x0 -> x11, Pallas kernels: none -> 6.81 us  [the longest x1 2.22 us: body(): call(backward, 'backward', shape((panels + 1, width, block), F32), [SMEM]...]
    unnamed x20 -> x18, local copies, waits for them, and re-layouts: 2.54 us -> 6.86 us
    dot_general x1 -> x0, local copies, waits for them, and re-layouts: 3.23 us -> none  [body(): jnp.einsum('psrc,prf->pscf', tiles[0], scaled.reshape(panels_dev, block,...]
    ppermute x4 -> x9, starting transfers between devices: 6.24 us -> 9.35 us  [the longest x2 4.12 us: swap_far(): lax.ppermute(block, 'cluster', [(c, (c + 1) % n if c % 2 else (c - 1) % n...]
  transfers between devices with their start and end apart: 5 -> 9, of which waited for: 2 -> 6; matrix products, arithmetic and copies ran while one was open for 3% -> 4% of each run, Pallas kernels for 0% -> 15%
where the time goes in v1:
time: 36.8 us; the launch traced here: 36.4 us
  waiting for transfers between devices  11.7 us (32%)
  starting transfers between devices  9.35 us (25%)
  local copies, waits for them, and re-layouts  6.87 us (19%)
  Pallas kernels  6.81 us (19%)
  other arithmetic  0.89 us (2%)
  between operations  0.75 us (2%)
    ppermute x5, waiting for transfers between devices, swap(): return lax.ppermute(block, 'cluster', [(c, c ^ c_flip) for c in range(nc)])  7.7 us
    unnamed x18, local copies, waits for them, and re-layouts  6.86 us
    ppermute x2, starting transfers between devices, swap_far(): lax.ppermute(block, 'cluster', [(c, (c + 1) % n if c % 2 else (c - 1) % n...  4.12 us
    ppermute x2, starting transfers between devices, swap(): return lax.ppermute(block, ('cluster', 'batch'), pairs)  3.81 us
    ppermute x2, waiting for transfers between devices, swap(): return lax.ppermute(block, ('cluster', 'batch'), pairs)  3.25 us
    pallas_call x1, Pallas kernels, body(): call(backward, 'backward', shape((panels + 1, width, block), F32), [SMEM]...  2.22 us
    pallas_call x1, Pallas kernels, body(): call(forward_near, 'forward_near', [shape((near, hidden), BF16), shape((h...  1.85 us
    ppermute x5, starting transfers between devices, swap(): return lax.ppermute(block, 'cluster', [(c, c ^ c_flip) for c in range(nc)])  1.42 us
  transfers between devices with their start and end apart: 9, of which 6 were waited for; matrix products, arithmetic and copies ran while one was open for 4% of the time, Pallas kernels for 15%

profile of v1, /device:TPU:0, one launch (start us, length us, event | category | flops | bytes accessed | tf_op | source)
XLA Modules:
  0.0 36.4 jit_solution(1756977371439024636)
XLA Ops:
  0.6 0.9 %select_bitcast_fusion = (bf16[256,128]{1,0:T(8,128)(2,1)S(1)}, bf16[256,128]{1,0:T(8,128)(2,1)S(1)}) fusion(pred[]{:T(512)S(6)} %eq.6, bf16[1,1024,128]{2,1,0:T(8,128)(2,1)} %feat.1), kind=kLoop, calls=%fused_computation | loop fusion | flops 65536 | bytes 262145 | tf_op jit(solution)/shard_map/jit(_where)/select_n | solution.py:295
  1.5 0.5 %collective-permute-start = (bf16[256,128]{1,0:T(8,128)(2,1)S(1)}, bf16[256,128]{1,0:T(8,128)(2,1)S(1)}, u32[]{:S(2)}, u32[]{:S(2)}) collective-permute-start(bf16[256,128]{1,0:T(8,128)(2,1)S(1)} %get-tuple-element.45), channel_id=1, source_target_pairs={{0,4},{4,0},{8,12},{12,8},{16,20},{20,16},{24,28},{28,24},{1,5},{5... | collective-permute-start | bytes 196616 | tf_op jit(solution)/shard_map/ppermute | solution.py:275
  2.0 3.6 %collective-permute-start.1 = (bf16[256,128]{1,0:T(8,128)(2,1)S(1)}, bf16[256,128]{1,0:T(8,128)(2,1)S(1)}, u32[]{:S(2)}, u32[]{:S(2)}) collective-permute-start(bf16[256,128]{1,0:T(8,128)(2,1)S(1)} %get-tuple-element.44), channel_id=1, source_target_pairs={{0,28},{4,8},{8,4},{12,16},{16,12},{20,24},{24,20},{28,0},{1,29},{... | collective-permute-start | bytes 196616 | tf_op jit(solution)/shard_map/ppermute | solution.py:282
  5.6 0.8 %copy.14.cols = s32[1,8,5]{2,1,0:T(8,128)S(1)} copy(s32[1,8,5]{1,0,2:T(1,128)} %param.10) | data formatting | bytes 320 | tf_op args[2]
  6.4 0.7 %copy.13.counts = s32[1,8,5,128]{3,2,1,0:T(8,128)S(1)} copy(s32[1,8,5,128]{3,1,2,0:T(8,128)} %param.12) | data formatting | bytes 40960 | tf_op args[4]
  7.1 0.0 collective-permute-done.mate
  7.1 0.0 copy-start
  7.1 1.3 %copy-done = bf16[1,8,5,128,128]{4,3,2,1,0:T(8,128)(2,1)S(1)} copy-done((bf16[1,8,5,128,128]{4,3,2,1,0:T(8,128)(2,1)S(1)}, bf16[1,8,5,128,128]{4,3,2,1,0:T(8,128)(2,1)}, u32[]{:S(2)}) %copy-start) | copy-done | bytes 1310744
  8.4 0.0 copy-start.2
  8.4 0.8 %copy-done.2 = bf16[256,128]{1,0:T(8,128)(2,1)S(1)} copy-done((bf16[256,128]{1,0:T(8,128)(2,1)S(1)}, bf16[256,128]{1,0:T(8,128)(2,1)}, u32[]{:S(2)}) %copy-start.2) | copy-done | bytes 65560
  9.3 0.0 copy-start.3
  9.3 0.9 %copy-done.3 = bf16[1,1024,128]{2,1,0:T(8,128)(2,1)S(1)} copy-done((bf16[1,1024,128]{2,1,0:T(8,128)(2,1)S(1)}, bf16[1,1024,128]{2,1,0:T(8,128)(2,1)}, u32[]{:S(2)}) %copy-start.3) | copy-done | bytes 262168
  10.2 0.0 copy-start.4
  10.2 0.9 %copy-done.4 = bf16[1,1024,128]{2,1,0:T(8,128)(2,1)S(1)} copy-done((bf16[1,1024,128]{2,1,0:T(8,128)(2,1)S(1)}, bf16[1,1024,128]{2,1,0:T(8,128)(2,1)}, u32[]{:S(2)}) %copy-start.4) | copy-done | bytes 262168
  11.2 0.0 copy-start.5
  11.2 0.7 %copy-done.5 = s32[1,8]{1,0:T(1,128)S(1)} copy-done((s32[1,8]{1,0:T(1,128)S(1)}, s32[1,8]{1,0:T(1,128)}, u32[]{:S(2)}) %copy-start.5) | copy-done | bytes 56
  11.8 0.0 copy-start.7
  11.8 0.7 %copy-done.7 = f32[128]{0:T(128)S(1)} copy-done((f32[128]{0:T(128)S(1)}, f32[128]{0:T(128)}, u32[]{:S(2)}) %copy-start.7) | copy-done | bytes 536
  12.5 1.9 %forward_near.1 = (bf16[768,128]{1,0:T(8,128)(2,1)S(1)}, bf16[128,768]{1,0:T(8,128)(2,1)S(1)}, f32[8,128]{1,0:T(8,128)S(1)}, bf16[256,256]{1,0:T(8,128)(2,1)S(1)...) custom-call(s32[1,8,5]{2,1,0:T(8,128)S(1)} %copy.14.cols, ...), custom_call_target="tpu_custom_call" | custom-call | flops 400000000 | bytes 4194304 | tf_op jit(solution)/shard_map/forward_near/pallas_call | solution.py:299
  14.3 0.0 copy-start.1
  14.4 0.0 copy-start.6
  14.4 0.0 collective-permute-done.1.halo
  14.4 0.5 %forward_far.1 = (bf16[256,128]{1,0:T(8,128)(2,1)S(1)}, bf16[128,256]{1,0:T(8,128)(2,1)S(1)}, f32[144,128]{1,0:T(8,128)S(1)}, bf16[400,128]{1,0:T(8,128)(2,1)S(1)}) custom-call(bf16[256,128]{1,0:T(8,128)(2,1)S(1)} %collective-permute-done.1.halo, bf16[256,256]{1,0:T(8,128)(2,1)S(1)} %get-tuple-element.25.t_far, f32[256,128]{1,0:T(8,128)S(1)} %get-tuple-element.26.s_far, ...), custom_call_target="tpu_custom_call" | custom-call | flops 100000000 | bytes 1048576 | tf_op jit(solution)/shard_map/forward_far/pallas_call | solution.py:322
  14.9 0.1 collective-permute-start.2
  15.0 1.3 %collective-permute-done.2.from_mate.got = bf16[400,128]{1,0:T(8,128)(2,1)S(1)} collective-permute-done((bf16[400,128]{1,0:T(8,128)(2,1)S(1)}, bf16[400,128]{1,0:T(8,128)(2,1)S(1)}, u32[]{:S(2)}, u32[]{:S(2)}) %collective-permute-start.2) | collective-permute-done | bytes 102432 | tf_op jit(solution)/shard_map/ppermute | solution.py:275
  16.3 0.3 collective-permute-start.4
  16.6 3.2 %collective-permute-done.4.got = bf16[144,128]{1,0:T(8,128)(2,1)S(1)} collective-permute-done((bf16[144,128]{1,0:T(8,128)(2,1)S(1)}, bf16[144,128]{1,0:T(8,128)(2,1)S(1)}, u32[]{:S(2)}, u32[]{:S(2)}) %collective-permute-start.4) | collective-permute-done | bytes 36896 | tf_op jit(solution)/shard_map/ppermute | solution.py:275
  19.9 0.3 collective-permute-start.5
  20.2 3.2 %collective-permute-done.5.got = bf16[144,128]{1,0:T(8,128)(2,1)S(1)} collective-permute-done((bf16[144,128]{1,0:T(8,128)(2,1)S(1)}, bf16[144,128]{1,0:T(8,128)(2,1)S(1)}, u32[]{:S(2)}, u32[]{:S(2)}) %collective-permute-start.5) | collective-permute-done | bytes 36896 | tf_op jit(solution)/shard_map/ppermute | solution.py:275
  23.4 1.4 %collective-permute-start.6 = (bf16[144,128]{1,0:T(8,128)(2,1)S(1)}, bf16[144,128]{1,0:T(8,128)(2,1)S(1)}, u32[]{:S(2)}, u32[]{:S(2)}) collective-permute-start(bf16[144,128]{1,0:T(8,128)(2,1)S(1)} %next_sum.5.mine), channel_id=1, source_target_pairs={{0,5},{1,4},{2,7},{3,6},{4,1},{5,0},{6,3},{7,2},{8,13},{9,12},{10,... | collective-permute-start | bytes 110600 | tf_op jit(solution)/shard_map/ppermute | solution.py:277
  24.8 2.1 %collective-permute-done.6.got = bf16[144,128]{1,0:T(8,128)(2,1)S(1)} collective-permute-done((bf16[144,128]{1,0:T(8,128)(2,1)S(1)}, bf16[144,128]{1,0:T(8,128)(2,1)S(1)}, u32[]{:S(2)}, u32[]{:S(2)}) %collective-permute-start.6) | collective-permute-done | bytes 36896 | tf_op jit(solution)/shard_map/ppermute | solution.py:277
  26.9 2.4 %collective-permute-start.7 = (bf16[144,128]{1,0:T(8,128)(2,1)S(1)}, bf16[144,128]{1,0:T(8,128)(2,1)S(1)}, u32[]{:S(2)}, u32[]{:S(2)}) collective-permute-start(bf16[144,128]{1,0:T(8,128)(2,1)S(1)} %next_sum.6.mine), channel_id=1, source_target_pairs={{0,6},{1,7},{2,4},{3,5},{4,2},{5,3},{6,0},{7,1},{8,14},{9,15},{10,... | collective-permute-start | bytes 110600 | tf_op jit(solution)/shard_map/ppermute | solution.py:277
  29.3 0.3 return_far.1
  29.6 0.6 %collective-permute-start.3 = (bf16[256,128]{1,0:T(8,128)(2,1)S(1)}, bf16[256,128]{1,0:T(8,128)(2,1)S(1)}, u32[]{:S(2)}, u32[]{:S(2)}) collective-permute-start(bf16[256,128]{1,0:T(8,128)(2,1)S(1)} %return_far.1), channel_id=1, source_target_pairs={{0,28},{4,8},{8,4},{12,16},{16,12},{20,24},{24,20},{28,0},{1,29},{... | collective-permute-start | bytes 196616 | tf_op jit(solution)/shard_map/ppermute | solution.py:282
  30.2 1.1 %collective-permute-done.7.got = bf16[144,128]{1,0:T(8,128)(2,1)S(1)} collective-permute-done((bf16[144,128]{1,0:T(8,128)(2,1)S(1)}, bf16[144,128]{1,0:T(8,128)(2,1)S(1)}, u32[]{:S(2)}, u32[]{:S(2)}) %collective-permute-start.7) | collective-permute-done | bytes 36896 | tf_op jit(solution)/shard_map/ppermute | solution.py:277
  31.4 0.2 collective-permute-start.8
  31.6 0.0 copy-done.1
  31.6 0.0 copy-done.6
  31.6 2.2 %backward.1.total = f32[9,128,128]{2,1,0:T(8,128)S(1)} custom-call(s32[1,8,5]{2,1,0:T(8,128)S(1)} %copy.14.cols, s32[1,8]{1,0:T(1,128)S(1)} %copy-done.6, bf16[1,8,5,128,128]{4,3,2,1,0:T(8,128)(2,1)S(1)} %copy-done.1, bf16[256,128]{1,0:T(8,128)(2,1)S(1)} %copy-done.2, bf16[128,768]{1,0:T(8,128)(2,1)S(1)} %get-tuple-element.24.near_t, ...), custom_call_target="tpu_custom_call" | custom-call | flops 400000000 | bytes 3145728 | tf_op jit(solution)/shard_map/backward/pallas_call | solution.py:341
  33.8 0.7 %collective-permute-done.3.from_far = bf16[256,128]{1,0:T(8,128)(2,1)S(1)} collective-permute-done((bf16[256,128]{1,0:T(8,128)(2,1)S(1)}, bf16[256,128]{1,0:T(8,128)(2,1)S(1)}, u32[]{:S(2)}, u32[]{:S(2)}) %collective-permute-start.3) | collective-permute-done | bytes 65568 | tf_op jit(solution)/shard_map/ppermute | solution.py:282
  34.6 1.0 %gather_outputs.1 = (f32[1,1024,128]{2,1,0:T(8,128)}, bf16[1,1024,128]{2,1,0:T(8,128)(2,1)}) custom-call(f32[9,128,128]{2,1,0:T(8,128)S(1)} %backward.1.total, bf16[400,128]{1,0:T(8,128)(2,1)S(1)} %collective-permute-done.2.from_mate.got, bf16[256,128]{1,0:T(8,128)(2,1)S(1)} %collective-permute-done.3.from_far, ...), custom_call_target="tpu_custom_call" | custom-call | flops 1000000 | bytes 2097152 | tf_op jit(solution)/shard_map/gather_outputs/pallas_call | solution.py:356
  35.6 0.0 collective-permute-done.8.got
  35.6 0.8 %finish.1 = (f32[256,128]{1,0:T(8,128)}, f32[1,128]{1,0:T(1,128)}) custom-call(f32[144,128]{1,0:T(8,128)S(1)} %next_sum.7.mine, f32[128,128]{1,0:T(8,128)S(1)} %collective-permute-done.8.got), custom_call_target="tpu_custom_call" | custom-call | flops 100000 | bytes 100000 | tf_op jit(solution)/shard_map/finish/pallas_call | solution.py:353
  (6 shorter events, 0.1 us)
Async XLA Ops:
  1.5 5.6 %collective-permute-start = (bf16[256,128]{1,0:T(8,128)(2,1)S(1)}, bf16[256,128]{1,0:T(8,128)(2,1)S(1)}, u32[]{:S(2)}, u32[]{:S(2)}) collective-permute-start(bf16[256,128]{1,0:T(8,128)(2,1)S(1)} %get-tuple-element.45), channel_id=1, source_target_pairs={{0,4},{4,0},{8,12},{12,8},{16,20},{20,16},{24,28},{28,24},{1,5},{5... | collective-permute-start | bytes 196616 | tf_op jit(solution)/shard_map/ppermute | solution.py:275
  2.0 12.3 %collective-permute-start.1 = (bf16[256,128]{1,0:T(8,128)(2,1)S(1)}, bf16[256,128]{1,0:T(8,128)(2,1)S(1)}, u32[]{:S(2)}, u32[]{:S(2)}) collective-permute-start(bf16[256,128]{1,0:T(8,128)(2,1)S(1)} %get-tuple-element.44), channel_id=1, source_target_pairs={{0,28},{4,8},{8,4},{12,16},{16,12},{20,24},{24,20},{28,0},{1,29},{... | collective-permute-start | bytes 196616 | tf_op jit(solution)/shard_map/ppermute | solution.py:282
  7.1 1.3 %copy-start = (bf16[1,8,5,128,128]{4,3,2,1,0:T(8,128)(2,1)S(1)}, bf16[1,8,5,128,128]{4,3,2,1,0:T(8,128)(2,1)}, u32[]{:S(2)}) copy-start(bf16[1,8,5,128,128]{4,3,2,1,0:T(8,128)(2,1)} %tiles.3) | copy-start | bytes 3932164
  8.4 0.8 %copy-start.2 = (bf16[256,128]{1,0:T(8,128)(2,1)S(1)}, bf16[256,128]{1,0:T(8,128)(2,1)}, u32[]{:S(2)}) copy-start(bf16[256,128]{1,0:T(8,128)(2,1)} %weight.7) | copy-start | bytes 196612
  9.3 0.9 %copy-start.3 = (bf16[1,1024,128]{2,1,0:T(8,128)(2,1)S(1)}, bf16[1,1024,128]{2,1,0:T(8,128)(2,1)}, u32[]{:S(2)}) copy-start(bf16[1,1024,128]{2,1,0:T(8,128)(2,1)} %feat.1) | copy-start | bytes 786436
  10.2 0.9 %copy-start.4 = (bf16[1,1024,128]{2,1,0:T(8,128)(2,1)S(1)}, bf16[1,1024,128]{2,1,0:T(8,128)(2,1)}, u32[]{:S(2)}) copy-start(bf16[1,1024,128]{2,1,0:T(8,128)(2,1)} %cot.1) | copy-start | bytes 786436
  11.2 0.7 %copy-start.5 = (s32[1,8]{1,0:T(1,128)S(1)}, s32[1,8]{1,0:T(1,128)}, u32[]{:S(2)}) copy-start(s32[1,8]{1,0:T(1,128)} %live.3) | copy-start | bytes 100
  11.8 0.7 %copy-start.7 = (f32[128]{0:T(128)S(1)}, f32[128]{0:T(128)}, u32[]{:S(2)}) copy-start(f32[128]{0:T(128)} %param.14) | copy-start | bytes 1540
  14.3 17.3 %copy-start.1 = (bf16[1,8,5,128,128]{4,3,2,1,0:T(8,128)(2,1)S(1)}, bf16[1,8,5,128,128]{4,3,2,1,0:T(8,128)(2,1)}, u32[]{:S(2)}) copy-start(bf16[1,8,5,128,128]{4,3,2,1,0:T(8,128)(2,1)} %tiles.3) | copy-start | bytes 3932164
  14.4 17.2 %copy-start.6 = (s32[1,8]{1,0:T(1,128)S(1)}, s32[1,8]{1,0:T(1,128)}, u32[]{:S(2)}) copy-start(s32[1,8]{1,0:T(1,128)} %live.3) | copy-start | bytes 100
  14.9 1.4 %collective-permute-start.2 = (bf16[400,128]{1,0:T(8,128)(2,1)S(1)}, bf16[400,128]{1,0:T(8,128)(2,1)S(1)}, u32[]{:S(2)}, u32[]{:S(2)}) collective-permute-start(bf16[400,128]{1,0:T(8,128)(2,1)S(1)} %get-tuple-element.36), channel_id=1, source_target_pairs={{0,4},{4,0},{8,12},{12,8},{16,20},{20,16},{24,28},{28,24},{1,5},{5... | collective-permute-start | bytes 307208 | tf_op jit(solution)/shard_map/ppermute | solution.py:275
  16.3 3.5 %collective-permute-start.4 = (bf16[144,128]{1,0:T(8,128)(2,1)S(1)}, bf16[144,128]{1,0:T(8,128)(2,1)S(1)}, u32[]{:S(2)}, u32[]{:S(2)}) collective-permute-start(bf16[144,128]{1,0:T(8,128)(2,1)S(1)} %first_sum.1.mine), channel_id=1, source_target_pairs={{0,12},{4,8},{8,4},{12,0},{16,28},{20,24},{24,20},{28,16},{1,13},{... | collective-permute-start | bytes 110600 | tf_op jit(solution)/shard_map/ppermute | solution.py:275
  19.9 3.5 %collective-permute-start.5 = (bf16[144,128]{1,0:T(8,128)(2,1)S(1)}, bf16[144,128]{1,0:T(8,128)(2,1)S(1)}, u32[]{:S(2)}, u32[]{:S(2)}) collective-permute-start(bf16[144,128]{1,0:T(8,128)(2,1)S(1)} %next_sum.4.mine), channel_id=1, source_target_pairs={{0,20},{4,16},{8,28},{12,24},{16,4},{20,0},{24,12},{28,8},{1,21},{... | collective-permute-start | bytes 110600 | tf_op jit(solution)/shard_map/ppermute | solution.py:275
  23.4 3.5 %collective-permute-start.6 = (bf16[144,128]{1,0:T(8,128)(2,1)S(1)}, bf16[144,128]{1,0:T(8,128)(2,1)S(1)}, u32[]{:S(2)}, u32[]{:S(2)}) collective-permute-start(bf16[144,128]{1,0:T(8,128)(2,1)S(1)} %next_sum.5.mine), channel_id=1, source_target_pairs={{0,5},{1,4},{2,7},{3,6},{4,1},{5,0},{6,3},{7,2},{8,13},{9,12},{10,... | collective-permute-start | bytes 110600 | tf_op jit(solution)/shard_map/ppermute | solution.py:277
  26.9 4.4 %collective-permute-start.7 = (bf16[144,128]{1,0:T(8,128)(2,1)S(1)}, bf16[144,128]{1,0:T(8,128)(2,1)S(1)}, u32[]{:S(2)}, u32[]{:S(2)}) collective-permute-start(bf16[144,128]{1,0:T(8,128)(2,1)S(1)} %next_sum.6.mine), channel_id=1, source_target_pairs={{0,6},{1,7},{2,4},{3,5},{4,2},{5,3},{6,0},{7,1},{8,14},{9,15},{10,... | collective-permute-start | bytes 110600 | tf_op jit(solution)/shard_map/ppermute | solution.py:277
  29.6 4.9 %collective-permute-start.3 = (bf16[256,128]{1,0:T(8,128)(2,1)S(1)}, bf16[256,128]{1,0:T(8,128)(2,1)S(1)}, u32[]{:S(2)}, u32[]{:S(2)}) collective-permute-start(bf16[256,128]{1,0:T(8,128)(2,1)S(1)} %return_far.1), channel_id=1, source_target_pairs={{0,28},{4,8},{8,4},{12,16},{16,12},{20,24},{24,20},{28,0},{1,29},{... | collective-permute-start | bytes 196616 | tf_op jit(solution)/shard_map/ppermute | solution.py:282
  31.4 4.2 %collective-permute-start.8 = (f32[128,128]{1,0:T(8,128)S(1)}, f32[128,128]{1,0:T(8,128)S(1)}, u32[]{:S(2)}, u32[]{:S(2)}) collective-permute-start(f32[128,128]{1,0:T(8,128)S(1)} %slice.12), channel_id=1, source_target_pairs={{0,4},{4,0},{8,12},{12,8},{16,20},{20,16},{24,28},{28,24},{1,5},{5... | collective-permute-start | bytes 196616 | tf_op jit(solution)/shard_map/ppermute | solution.py:275

commit v2 on v1

--- a/solution.py
+++ b/solution.py
@@ -13,6 +13,8 @@
 F32 = jnp.float32
 BF16 = jnp.bfloat16
 VMEM = pl.BlockSpec(memory_space=pltpu.VMEM)
+ANY = pl.BlockSpec(memory_space=pl.ANY)
+HBM = pl.BlockSpec(memory_space=pltpu.HBM)
 SMEM = pl.BlockSpec(memory_space=pltpu.SMEM)
 
 
@@ -71,7 +73,7 @@
         for m in range(REACH):
             found = jnp.int32(0)
             for s in range(slots):
-                hit = (s < live[0, p]) & (cols[0, p, s] - first == outside + m)
+                hit = (s < live[0, p]) & (cols[s, 0, p] - first == outside + m)
                 found = found + jnp.where(hit, s + 1, 0)
             tile = tiles[0, p, jnp.maximum(found - 1, 0)]
             blocks.append(jnp.where(found > 0, tile, jnp.zeros_like(tile)))
@@ -80,8 +82,21 @@
 
 
 def own_slot(cols, live, p, s, first, panels):
-    q = cols[0, p, s] - first
+    q = cols[s, 0, p] - first
     return jnp.where((s < live[0, p]) & (q >= 0) & (q < panels), q, panels)
+
+
+def pick_halo(feat, far_rows, mate_rows, sems):
+    nodes, span = feat.shape[1], far_rows.shape[0]
+    par = lax.axis_index("cluster") % 2
+    starts = ((nodes - span) * par, (nodes - span) * (1 - par))
+    copies = []
+    for i, (start, rows) in enumerate(zip(starts, (far_rows, mate_rows))):
+        source = feat.at[0, pl.ds(pl.multiple_of(start, span), span), :]
+        copies.append(pltpu.make_async_copy(source, rows, sems.at[i]))
+        copies[-1].start()
+    for copy in copies:
+        copy.wait()
 
 
 def forward_near(
@@ -99,13 +114,20 @@
     span = REACH * block
     own[0 : panels * block, :] = feat[0]
     own[panels * block :, :] = jnp.zeros((block, width), BF16)
-    rows = []
-    for p in order:
-        count = counts[0, p]
-        slot = lax.broadcasted_iota(jnp.int32, count.shape, 0)
-        kept = jnp.where(slot < live[0, p], count, 0).astype(F32)
-        rows.append(jnp.sum(kept, axis=0, keepdims=True))
-    recip_rows = 1.0 / jnp.concatenate(rows, axis=0)
+    row = lax.broadcasted_iota(jnp.int32, (panels, block), 0)
+    depth = jnp.zeros((panels, block), jnp.int32)
+    for p in range(panels):
+        depth = jnp.where(row == p, live[0, p], depth)
+    degree = jnp.zeros((panels, block), jnp.int32)
+    for s in range(slots):
+        degree = degree + jnp.where(depth > s, counts[0, s], 0)
+    inverse = 1.0 / degree.astype(F32)
+    low, middle, high = inverse[:REACH], inverse[REACH : panels - REACH], inverse[panels - REACH :]
+    recip_rows = jnp.where(
+        par == 0,
+        jnp.concatenate([middle, high, low], axis=0),
+        jnp.concatenate([middle, low, high], axis=0),
+    )
     recip[...] = recip_rows
     recip_cols = recip_rows.T
 
@@ -189,54 +211,76 @@
         far_ret[m * block : (m + 1) * block, :] = back[:, m * block : (m + 1) * block]
 
 
-def first_sum(kept, got, total):
+def first_sum(kept, got, far_ret, total, far_out):
     rows = kept.shape[0] - TAIL
+    far_out[...] = far_ret[...]
     total[0:rows, :] = (kept[0:rows, :] + got[0:rows, :].astype(F32)).astype(BF16)
     total[rows:, :] = tail_rows(kept[rows : rows + 1, :] + tail_total(got[rows : rows + TAIL, :]))
 
 
 def next_sum(mine, got, total):
     rows = mine.shape[0] - TAIL
-    total[0:rows, :] = (mine[0:rows, :].astype(F32) + got[0:rows, :].astype(F32)).astype(total.dtype)
+    total[0:rows, :] = (mine[0:rows, :].astype(F32) + got[0:rows, :].astype(F32)).astype(BF16)
+    total[rows:, :] = tail_rows(tail_total(mine[rows:, :]) + tail_total(got[rows:, :]))
+
+
+def last_sum(mine, got, total):
+    rows = mine.shape[0] - TAIL
+    total[0:rows, :] = mine[0:rows, :].astype(F32) + got[0:rows, :].astype(F32)
     b_total = tail_total(mine[rows:, :]) + tail_total(got[rows:, :])
-    if total.dtype == BF16:
-        total[rows:, :] = tail_rows(b_total)
-    else:
-        total[rows:, :] = jnp.broadcast_to(b_total, (TAIL, b_total.shape[1]))
+    total[rows:, :] = jnp.broadcast_to(b_total, (total.shape[0] - rows, b_total.shape[1]))
 
 
 def finish(mine, got, grad, grad_bias, *, clusters, batches, scale):
     half = half_of(clusters, batches)
-    rows = got.shape[0]
+    rows = grad.shape[0] // 2
     own = mine[0:rows, :].T * scale
-    other = got[...].T * scale
+    other = got[0:rows, :].T * scale
     grad[0:rows, :] = jnp.where(half == 0, own, other)
     grad[rows:, :] = jnp.where(half == 0, other, own)
-    grad_bias[...] = mine[rows : rows + 1, :] * scale
-
-
-def backward(cols, live, tiles, weight, near_t, far_t, recip, total):
+    grad_bias[...] = jnp.where(half == 0, mine[rows : rows + 1, :], got[rows : rows + 1, :]) * scale
+
+
+def spread(cols, live, tiles, weight, parts, recip, total, panel_list, first_row):
     panels, slots, block = tiles.shape[1], tiles.shape[2], tiles.shape[3]
     width = weight.shape[1]
     first = lax.axis_index("cluster") * panels
+    for j, p in enumerate(panel_list):
+        row = recip[first_row + j : first_row + j + 1, :]
+        scaled = (dot(weight[width:, :], parts[j]) * row).astype(BF16)
+        terms = dot(scaled, jnp.concatenate([tiles[0, p, s] for s in range(slots)], axis=1))
+        for s in range(slots):
+            q = own_slot(cols, live, p, s, first, panels)
+            total[q] = total[q] + terms[:, s * block : (s + 1) * block]
+
+
+def backward_mid(cols, live, tiles, weight, near_t, far_t, recip, total):
+    panels, block = tiles.shape[1], tiles.shape[3]
+    width = weight.shape[1]
     edge, far, _ = edges(panels)
     mid = panels - 2 * REACH
+    parts = [near_t[:, j * block : (j + 1) * block] for j in range(mid + REACH)]
+    parts += [far_t[:, j * block : (j + 1) * block] for j in range(REACH)]
     order = [REACH + j for j in range(mid)] + [edge + j for j in range(REACH)] + [far + j for j in range(REACH)]
-    near = mid + REACH
-    parts = [near_t[:, j * block : (j + 1) * block] for j in range(near)]
-    parts += [far_t[:, j * block : (j + 1) * block] for j in range(REACH)]
     for j, p in enumerate(order):
         total[p] = dot(weight[:width, :], parts[j])
     total[panels] = jnp.zeros((width, block), F32)
-    for j, p in enumerate(order):
-        scaled = (dot(weight[width:, :], parts[j]) * recip[j : j + 1, :]).astype(BF16)
-        spread = dot(scaled, jnp.concatenate([tiles[0, p, s] for s in range(slots)], axis=1))
-        for s in range(slots):
-            q = own_slot(cols, live, p, s, first, panels)
-            total[q] = total[q] + spread[:, s * block : (s + 1) * block]
-
-
-def gather_outputs(total, from_mate, from_far, out_near, out_far, grad, output):
+    spread(cols, live, tiles, weight, parts, recip, total, order[:mid], 0)
+
+
+def backward_rim(cols, live, tiles, weight, near_t, far_t, recip, before, total):
+    panels, block = tiles.shape[1], tiles.shape[3]
+    edge, far, _ = edges(panels)
+    mid = panels - 2 * REACH
+    parts = [near_t[:, j * block : (j + 1) * block] for j in range(mid, mid + REACH)]
+    parts += [far_t[:, j * block : (j + 1) * block] for j in range(REACH)]
+    total[...] = before[...]
+    order = [edge + j for j in range(REACH)] + [far + j for j in range(REACH)]
+    spread(cols, live, tiles, weight, parts, recip, total, order, mid)
+
+
+def gather_outputs(total, from_mate, from_far, out_near, out_far, grad, output, token):
+    token[...] = jnp.zeros(token.shape, F32)
     panels, block = total.shape[0] - 1, total.shape[2]
     edge, far, _ = edges(panels)
     mid = panels - 2 * REACH
@@ -254,32 +298,51 @@
     output[0, pl.ds(pl.multiple_of(far * block, block), REACH * block), :] = out_far[...]
 
 
-def call(kernel, name, shapes, specs, scratch=(), flops=0, nbytes=0, **static):
+def call(kernel, name, shapes, specs, scratch=(), micros=1.0, after=0, **static):
     single = not isinstance(shapes, (list, tuple))
-    body = functools.partial(kernel, **static) if static else kernel
+    inputs = len(specs)
+
+    def ordered(*refs):
+        kernel(*refs[:inputs], *refs[inputs + after :], **static)
+
     return pl.pallas_call(
-        body,
+        ordered,
         out_shape=shapes,
-        in_specs=specs,
+        in_specs=list(specs) + [ANY] * after,
         out_specs=VMEM if single else [VMEM] * len(shapes),
         scratch_shapes=list(scratch),
         compiler_params=pltpu.CompilerParams(vmem_limit_bytes=24 << 20),
-        cost_estimate=pl.CostEstimate(flops=flops, bytes_accessed=nbytes, transcendentals=0),
+        cost_estimate=pl.CostEstimate(flops=int(micros * 10**9), bytes_accessed=1 << 16, transcendentals=0),
         name=name,
     )
 
 
-def swap(block, c_flip, b_flip):
+def swap_chip(block):
+    nc = lax.axis_size("cluster")
+    return lax.ppermute(block, "cluster", [(c, c ^ 1) for c in range(nc)])
+
+
+def swap_flips(block, flips):
     nc, nb = lax.axis_size("cluster"), lax.axis_size("batch")
-    if b_flip == 0:
-        return lax.ppermute(block, "cluster", [(c, c ^ c_flip) for c in range(nc)])
-    pairs = [(c * nb + b, (c ^ c_flip) * nb + (b ^ b_flip)) for c in range(nc) for b in range(nb)]
+    pairs = []
+    for c in range(nc):
+        for b in range(nb):
+            c_flip, b_flip = flips[(c.bit_count() + b.bit_count()) % 2]
+            pairs.append((c * nb + b, (c ^ c_flip ^ 1) * nb + (b ^ b_flip)))
     return lax.ppermute(block, ("cluster", "batch"), pairs)
 
 
 def swap_far(block):
-    n = lax.axis_size("cluster")
-    return lax.ppermute(block, "cluster", [(c, (c + 1) % n if c % 2 else (c - 1) % n) for c in range(n)])
+    nc, nb = lax.axis_size("cluster"), lax.axis_size("batch")
+    pairs = []
+    for c in range(nc):
+        for b in range(nb):
+            other = c + 1 if c % 2 else c - 1
+            if 0 <= other < nc:
+                pairs.append((c * nb + b, other * nb + b))
+            else:
+                pairs.append((c * nb + b, c * nb + (b ^ 1)))
+    return lax.ppermute(block, ("cluster", "batch"), pairs)
 
 
 def body(features, tiles, columns, live_blocks, edge_counts, weight, bias, cotangent):
@@ -289,13 +352,22 @@
     nc, nb = lax.axis_size("cluster"), lax.axis_size("batch")
     span = REACH * block
     near = nodes - span
+    rows = hidden + TAIL
     shape = jax.ShapeDtypeStruct
-    par = lax.axis_index("cluster") % 2
-    low, high = features[0, :span], features[0, nodes - span :]
-    far_halo = swap_far(jnp.where(par == 0, low, high))
-    mate_halo = swap(jnp.where(par == 0, high, low), 1, 0)
+    sizes = dict(clusters=nc, batches=nb)
+    columns = jnp.transpose(columns, (2, 0, 1))
+    edge_counts = jnp.transpose(edge_counts, (0, 2, 1, 3))
     bias_row = bias.reshape(1, hidden)
-    sizes = dict(clusters=nc, batches=nb)
+    far_rows, mate_rows = call(
+        pick_halo,
+        "pick_halo",
+        [shape((span, width), BF16)] * 2,
+        [HBM],
+        [pltpu.SemaphoreType.DMA((2,))],
+        micros=8.0,
+    )(features)
+    mate_halo = swap_chip(mate_rows)
+    far_halo = swap_far(far_rows)
     (out_near, near_t, recip, t_far, s_far, r_far, p_far, c_far, f_far, w_part, b_part, mate_ret) = call(
         forward_near,
         "forward_near",
@@ -315,10 +387,8 @@
         ],
         [SMEM, SMEM] + [VMEM] * 7,
         [pltpu.VMEM((nodes + block, width), BF16)],
-        flops=4 * 10**8,
-        nbytes=4 << 20,
+        micros=2.0,
     )(columns, live_blocks, features, mate_halo, tiles, edge_counts, weight, bias_row, cotangent)
-    rows = hidden + TAIL
     out_far, far_t, kept, send = call(
         forward_far,
         "forward_far",
@@ -329,39 +399,67 @@
             shape((rows + span, width), BF16),
         ],
         [VMEM] * 11,
-        flops=10**8,
-        nbytes=1 << 20,
         **sizes,
     )(far_halo, t_far, s_far, r_far, p_far, c_far, f_far, weight, w_part, b_part, mate_ret)
-    got = swap(send, 1, 0)
-    far_ret = call(return_far, "return_far", shape((span, block), BF16), [VMEM] * 4, flops=10**7, nbytes=1 << 18)(
+    got = swap_chip(send)
+    far_ret = call(return_far, "return_far", shape((span, block), BF16), [VMEM] * 4, micros=0.3)(
         weight, far_t, t_far, recip
     )
-    from_far = swap_far(far_ret)
-    total = call(backward, "backward", shape((panels + 1, width, block), F32), [SMEM] * 2 + [VMEM] * 5, flops=4 * 10**8, nbytes=3 << 20)(
-        columns, live_blocks, tiles, weight, near_t, far_t, recip
-    )
-    mine = call(first_sum, "first_sum", shape((rows, width), BF16), [VMEM] * 2, flops=10**5, nbytes=10**5)(kept, got)
-    steps = [((1 << i) | 1, 0) for i in range(1, (nc - 1).bit_length())]
-    steps += [(1, 1 << i) for i in range((nb - 1).bit_length())]
-    for i, (c_flip, b_flip) in enumerate(steps):
-        other = swap(mine, c_flip, b_flip)
-        kind = F32 if i == len(steps) - 1 else BF16
-        mine = call(next_sum, "next_sum", shape((rows, width), kind), [VMEM] * 2, flops=10**5, nbytes=10**5)(mine, other)
-    last = swap(mine[:hidden], 1, 0)
+    mine, far_ret = call(
+        first_sum, "first_sum", [shape((rows, width), BF16), shape((span, block), BF16)], [VMEM] * 3, micros=0.1
+    )(kept, got, far_ret)
+    made = {}
+
+    def exchange_far(mine):
+        made["from_far"] = swap_far(far_ret)
+        return ()
+
+    def sum_mid(mine):
+        made["total"] = call(
+            backward_mid, "backward_mid", shape((panels + 1, width, block), F32), [SMEM] * 2 + [VMEM] * 5, micros=1.2, after=1
+        )(columns, live_blocks, tiles, weight, near_t, far_t, recip, mine)
+        return (made["total"],)
+
+    def sum_rim(mine):
+        made["total"] = call(
+            backward_rim, "backward_rim", shape((panels + 1, width, block), F32), [SMEM] * 2 + [VMEM] * 6, micros=1.2, after=1
+        )(columns, live_blocks, tiles, weight, near_t, far_t, recip, made["total"], mine)
+        return (made["total"],)
+
+    def write_outputs(mine):
+        grad_features, output, token = call(
+            gather_outputs,
+            "gather_outputs",
+            [shape((1, nodes, width), F32), shape((1, nodes, hidden), BF16), shape((8, hidden), F32)],
+            [VMEM] * 5,
+            after=1,
+        )(made["total"], got, made["from_far"], out_near, out_far, mine)
+        made["outputs"] = output, grad_features
+        return (token,)
+
+    tasks = [exchange_far, sum_mid, sum_rim, write_outputs]
+    bits = [(1 << i, 0) for i in range(1, (nc - 1).bit_length())] + [(0, 1 << i) for i in range((nb - 1).bit_length())]
+    turn = len(bits) // 2
+    steps = list(zip(bits, bits[turn:] + bits[:turn]))
+    for i, flips in enumerate(steps):
+        other = swap_flips(mine, flips)
+        held = tasks.pop(0)(mine) if tasks else ()
+        if i < len(steps) - 1:
+            mine = call(next_sum, "next_sum", shape((rows, width), BF16), [VMEM] * 2, micros=0.1, after=len(held))(
+                mine, other, *held
+            )
+        else:
+            mine = call(
+                last_sum, "last_sum", shape((hidden + 8, width), F32), [VMEM] * 2, micros=0.1, after=len(held)
+            )(mine, other, *held)
+    for task in tasks:
+        task(mine)
+    last = swap_chip(mine)
     scale = 1.0 / math.sqrt(nb * nc * nodes)
     grad_weight, grad_bias = call(
-        finish, "finish", [shape((2 * width, hidden), F32), shape((1, hidden), F32)], [VMEM] * 2, flops=10**5, nbytes=10**5, scale=scale, **sizes
+        finish, "finish", [shape((2 * width, hidden), F32), shape((1, hidden), F32)], [VMEM] * 2, scale=scale, **sizes
     )(mine, last)
-    grad_features, output = call(
-        gather_outputs,
-        "gather_outputs",
-        [shape((1, nodes, width), F32), shape((1, nodes, hidden), BF16)],
-        [VMEM] * 5,
-        flops=10**6,
-        nbytes=2 << 20,
-    )(total, got, from_far, out_near, out_far)
-    return output, grad_features, grad_weight, grad_bias.reshape(hidden)
+    return *made["outputs"], grad_weight, grad_bias.reshape(hidden)
 
 
 def solution(mesh):

time: 36.8 us -> 27.2 us (0.74)
  waiting for transfers between devices: 11.7 us -> 5.38 us
  local copies, waits for them, and re-layouts: 6.87 us -> 1.07 us
  starting transfers between devices: 9.35 us -> 12.1 us
  Pallas kernels: 6.81 us -> 7.73 us
  other arithmetic: 0.89 us -> 0 us
    ppermute x9, waiting for transfers between devices: 11.7 us -> 5.38 us  [the longest x4 3.01 us: swap_flips(): return lax.ppermute(block, ('cluster', 'batch'), pairs)]
    unnamed x18 -> x16, local copies, waits for them, and re-layouts: 6.86 us -> 1.07 us
    ppermute x9, starting transfers between devices: 9.35 us -> 12.1 us  [the longest x4 8.58 us: swap_flips(): return lax.ppermute(block, ('cluster', 'batch'), pairs)]
    pallas_call x8 -> x10, Pallas kernels: 3.67 us -> 4.57 us  [the longest x1 1.5 us: sum_mid(): call(backward_mid, 'backward_mid', shape((panels + 1, width, block), F32)...]
    select_n x1 -> x0, other arithmetic: 0.89 us -> none  [body(): far_halo = swap_far(jnp.where(par == 0, low, high))]
  transfers between devices with their start and end apart: 9 -> 9, of which waited for: 6 -> 7; matrix products, arithmetic and copies ran while one was open for 4% -> 0% of each run, Pallas kernels for 15% -> 23%
where the time goes in v2:
time: 27.2 us; the launch traced here: 27.1 us
  starting transfers between devices  12.1 us (44%)
  Pallas kernels  7.73 us (28%)
  waiting for transfers between devices  5.38 us (20%)
  local copies, waits for them, and re-layouts  1.07 us (4%)
  between operations  0.77 us (3%)
    ppermute x4, starting transfers between devices, swap_flips(): return lax.ppermute(block, ('cluster', 'batch'), pairs)  8.58 us
    ppermute x4, waiting for transfers between devices, swap_flips(): return lax.ppermute(block, ('cluster', 'batch'), pairs)  3.01 us
    ppermute x2, starting transfers between devices, swap_far(): return lax.ppermute(block, ('cluster', 'batch'), pairs)  2.65 us
    ppermute x3, waiting for transfers between devices, swap_chip(): return lax.ppermute(block, 'cluster', [(c, c ^ 1) for c in range(nc)])  2.05 us
    pallas_call x1, Pallas kernels, body(): call(forward_near, 'forward_near', [shape((near, hidden), BF16), shape((h...  1.87 us
    pallas_call x1, Pallas kernels, sum_mid(): call(backward_mid, 'backward_mid', shape((panels + 1, width, block), F32)...  1.5 us
    pallas_call x1, Pallas kernels, sum_rim(): call(backward_rim, 'backward_rim', shape((panels + 1, width, block), F32)...  1.41 us
    unnamed x16, local copies, waits for them, and re-layouts  1.07 us
  transfers between devices with their start and end apart: 9, of which 7 were waited for; matrix products, arithmetic and copies ran while one was open for 0% of the time, Pallas kernels for 23%

profile of v2, /device:TPU:0, one launch (start us, length us, event | category | flops | bytes accessed | tf_op | source)
XLA Modules:
  0.0 27.1 jit_solution(11197292290522860251)
XLA Ops:
  0.6 0.0 copy-start
  0.6 0.0 copy-start.1
  0.7 1.0 %copy-done.1 = bf16[1,1024,128]{2,1,0:T(8,128)(2,1)S(1)} copy-done((bf16[1,1024,128]{2,1,0:T(8,128)(2,1)S(1)}, bf16[1,1024,128]{2,1,0:T(8,128)(2,1)}, u32[]{:S(2)}) %copy-start.1) | copy-done | bytes 262168
  1.7 0.0 copy-start.2
  1.7 0.0 copy-start.3
  1.7 0.0 copy-start.4
  1.7 0.0 copy-start.5
  1.7 0.0 copy-start.6
  1.7 0.0 copy-start.7
  1.7 0.2 pick_halo.1
  1.9 0.5 %collective-permute-start = (bf16[256,128]{1,0:T(8,128)(2,1)S(1)}, bf16[256,128]{1,0:T(8,128)(2,1)S(1)}, u32[]{:S(2)}, u32[]{:S(2)}) collective-permute-start(bf16[256,128]{1,0:T(8,128)(2,1)S(1)} %get-tuple-element.29), channel_id=1, source_target_pairs={{0,4},{4,0},{8,12},{12,8},{16,20},{20,16},{24,28},{28,24},{1,5},{5... | collective-permute-start | bytes 196616 | tf_op jit(solution)/shard_map/ppermute | solution.py:322
  2.5 2.6 %collective-permute-start.1 = (bf16[256,128]{1,0:T(8,128)(2,1)S(1)}, bf16[256,128]{1,0:T(8,128)(2,1)S(1)}, u32[]{:S(2)}, u32[]{:S(2)}) collective-permute-start(bf16[256,128]{1,0:T(8,128)(2,1)S(1)} %get-tuple-element.31), channel_id=1, source_target_pairs={{0,1},{1,0},{2,3},{3,2},{4,8},{5,9},{6,10},{7,11},{8,4},{9,5},{10,... | collective-permute-start | bytes 196616 | tf_op jit(solution)/shard_map/ppermute | solution.py:345
  5.1 0.0 collective-permute-done.refs_3_
  5.1 0.0 copy-done
  5.1 0.0 copy-done.2
  5.1 0.0 copy-done.3
  5.1 0.0 copy-done.4
  5.1 0.0 copy-done.5
  5.2 0.0 copy-done.6
  5.2 0.0 copy-done.7
  5.2 1.9 %forward_near.1 = (bf16[768,128]{1,0:T(8,128)(2,1)S(1)}, bf16[128,768]{1,0:T(8,128)(2,1)S(1)}, f32[8,128]{1,0:T(8,128)S(1)}, bf16[256,256]{1,0:T(8,128)(2,1)S(1)...) custom-call(s32[5,1,8]{2,1,0:T(1,128)S(1)} %bitcast.5, ...), custom_call_target="tpu_custom_call" | custom-call | flops 2000000000 | bytes 65536 | tf_op jit(solution)/shard_map/forward_near/pallas_call | solution.py:371
  7.0 0.3 %collective-permute-done.1.refs_0_ = bf16[256,128]{1,0:T(8,128)(2,1)S(1)} collective-permute-done((bf16[256,128]{1,0:T(8,128)(2,1)S(1)}, bf16[256,128]{1,0:T(8,128)(2,1)S(1)}, u32[]{:S(2)}, u32[]{:S(2)}) %collective-permute-start.1) | collective-permute-done | bytes 65568 | tf_op jit(solution)/shard_map/ppermute | solution.py:345
  7.4 0.5 %forward_far.1 = (bf16[256,128]{1,0:T(8,128)(2,1)S(1)}, bf16[128,256]{1,0:T(8,128)(2,1)S(1)}, f32[144,128]{1,0:T(8,128)S(1)}, bf16[400,128]{1,0:T(8,128)(2,1)S(1)}) custom-call(bf16[256,128]{1,0:T(8,128)(2,1)S(1)} %collective-permute-done.1.refs_0_, bf16[256,256]{1,0:T(8,128)(2,1)S(1)} %get-tuple-element.32.refs_1_.refs_2_, ...), custom_call_target="tpu_custom_call" | custom-call | flops 1000000000 | bytes 65536 | tf_op jit(solution)/shard_map/forward_far/pallas_call | solution.py:392
  7.9 0.1 collective-permute-start.2
  8.0 0.3 %return_far.1.refs_2_ = bf16[256,128]{1,0:T(8,128)(2,1)S(1)} custom-call(bf16[256,128]{1,0:T(8,128)(2,1)S(1)} %copy-done.3, bf16[128,256]{1,0:T(8,128)(2,1)S(1)} %get-tuple-element.41.refs_1_.refs_5_, bf16[256,256]{1,0:T(8,128)(2,1)S(1)} %get-tuple-element.32.refs_1_.refs_2_, f32[8,128]{1,0:T(8,128)S(1)} %get-tuple-element.42.refs_3_.refs_6_), custom_call_target="tpu_custom_call" | custom-call | flops 300000000 | bytes 65536 | tf_op jit(solution)/shard_map/return_far/pallas_call | solution.py:405
  8.3 1.0 %collective-permute-done.2.refs_1_ = bf16[400,128]{1,0:T(8,128)(2,1)S(1)} collective-permute-done((bf16[400,128]{1,0:T(8,128)(2,1)S(1)}, bf16[400,128]{1,0:T(8,128)(2,1)S(1)}, u32[]{:S(2)}, u32[]{:S(2)}) %collective-permute-start.2) | collective-permute-done | bytes 102432 | tf_op jit(solution)/shard_map/ppermute | solution.py:322
  9.3 2.5 %collective-permute-start.3 = (bf16[144,128]{1,0:T(8,128)(2,1)S(1)}, bf16[144,128]{1,0:T(8,128)(2,1)S(1)}, u32[]{:S(2)}, u32[]{:S(2)}) collective-permute-start(bf16[144,128]{1,0:T(8,128)(2,1)S(1)} %get-tuple-element.45.refs_0_), channel_id=1, source_target_pairs={{0,12},{1,4},{2,7},{3,15},{4,1},{5,9},{6,10},{7,2},{8,13},{9,5},{1... | collective-permute-start | bytes 110600 | tf_op jit(solution)/shard_map/ppermute | solution.py:332
  11.8 0.0 collective-permute-start.5
  11.8 1.6 %collective-permute-done.3.refs_1_ = bf16[144,128]{1,0:T(8,128)(2,1)S(1)} collective-permute-done((bf16[144,128]{1,0:T(8,128)(2,1)S(1)}, bf16[144,128]{1,0:T(8,128)(2,1)S(1)}, u32[]{:S(2)}, u32[]{:S(2)}) %collective-permute-start.3) | collective-permute-done | bytes 36896 | tf_op jit(solution)/shard_map/ppermute | solution.py:332
  13.5 1.4 %collective-permute-start.4 = (bf16[144,128]{1,0:T(8,128)(2,1)S(1)}, bf16[144,128]{1,0:T(8,128)(2,1)S(1)}, u32[]{:S(2)}, u32[]{:S(2)}) collective-permute-start(bf16[144,128]{1,0:T(8,128)(2,1)S(1)} %next_sum.3.refs_7_.refs_0_), channel_id=1, source_target_pairs={{0,20},{1,7},{2,4},{3,23},{4,2},{5,17},{6,18},{7,1},{8,14},{9,29},... | collective-permute-start | bytes 110600 | tf_op jit(solution)/shard_map/ppermute | solution.py:332
  14.9 1.5 %backward_mid.1.refs_2_.refs_7_ = f32[9,128,128]{2,1,0:T(8,128)S(1)} custom-call(s32[5,1,8]{2,1,0:T(1,128)S(1)} %bitcast.6, s32[1,8]{1,0:T(1,128)S(1)} %copy-done.7, bf16[1,8,5,128,128]{4,3,2,1,0:T(8,128)(2,1)S(1)} %copy-done, bf16[256,128]{1,0:T(8,128)(2,1)S(1)} %copy-done.3, bf16[128,768]{1,0:T(8,128)(2,1)S(1)} %get-tuple-element.30.refs_4_, ...), custom_call_target="tpu_custom_call" | custom-call | flops 1200000000 | bytes 65536 | tf_op jit(solution)/shard_map/backward_mid/pallas_call | solution.py:418
  16.4 0.5 %collective-permute-done.4.refs_1_ = bf16[144,128]{1,0:T(8,128)(2,1)S(1)} collective-permute-done((bf16[144,128]{1,0:T(8,128)(2,1)S(1)}, bf16[144,128]{1,0:T(8,128)(2,1)S(1)}, u32[]{:S(2)}, u32[]{:S(2)}) %collective-permute-start.4) | collective-permute-done | bytes 36896 | tf_op jit(solution)/shard_map/ppermute | solution.py:332
  17.0 1.9 %collective-permute-start.6 = (bf16[144,128]{1,0:T(8,128)(2,1)S(1)}, bf16[144,128]{1,0:T(8,128)(2,1)S(1)}, u32[]{:S(2)}, u32[]{:S(2)}) collective-permute-start(bf16[144,128]{1,0:T(8,128)(2,1)S(1)} %next_sum.4.refs_8_.refs_0_), channel_id=1, source_target_pairs={{0,5},{1,13},{2,14},{3,6},{4,8},{5,0},{6,3},{7,11},{8,4},{9,12},{1... | collective-permute-start | bytes 110600 | tf_op jit(solution)/shard_map/ppermute | solution.py:332
  18.8 1.4 %backward_rim.1.refs_2_.refs_0_ = f32[9,128,128]{2,1,0:T(8,128)S(1)} custom-call(s32[5,1,8]{2,1,0:T(1,128)S(1)} %bitcast.7, s32[1,8]{1,0:T(1,128)S(1)} %copy-done.7, bf16[1,8,5,128,128]{4,3,2,1,0:T(8,128)(2,1)S(1)} %copy-done, bf16[256,128]{1,0:T(8,128)(2,1)S(1)} %copy-done.3, bf16[128,768]{1,0:T(8,128)(2,1)S(1)} %get-tuple-element.30.refs_4_, ...), custom_call_target="tpu_custom_call" | custom-call | flops 1200000000 | bytes 65536 | tf_op jit(solution)/shard_map/backward_rim/pallas_call | solution.py:424
  20.2 0.2 collective-permute-done.6.refs_1_
  20.5 2.8 %collective-permute-start.7 = (bf16[144,128]{1,0:T(8,128)(2,1)S(1)}, bf16[144,128]{1,0:T(8,128)(2,1)S(1)}, u32[]{:S(2)}, u32[]{:S(2)}) collective-permute-start(bf16[144,128]{1,0:T(8,128)(2,1)S(1)} %next_sum.5.refs_5_.refs_0_), channel_id=1, source_target_pairs={{0,6},{1,21},{2,22},{3,5},{4,16},{5,3},{6,0},{7,19},{8,28},{9,15},... | collective-permute-start | bytes 110600 | tf_op jit(solution)/shard_map/ppermute | solution.py:332
  23.3 0.0 collective-permute-done.5.refs_2_
  23.3 1.0 %gather_outputs.1 = (f32[1,1024,128]{2,1,0:T(8,128)}, bf16[1,1024,128]{2,1,0:T(8,128)(2,1)}, f32[8,128]{1,0:T(8,128)S(1)}) custom-call(f32[9,128,128]{2,1,0:T(8,128)S(1)} %backward_rim.1.refs_2_.refs_0_, bf16[400,128]{1,0:T(8,128)(2,1)S(1)} %collective-permute-done.2.refs_1_, bf16[256,128]{1,0:T(8,128)(2,1)S(1)} %collective-permute-done.5.refs_2_, ...), custom_call_target="tpu_custom_call" | custom-call | flops 1000000000 | bytes 65536 | tf_op jit(solution)/shard_map/gather_outputs/pallas_call | solution.py:430
  24.3 0.6 %collective-permute-done.7.refs_1_ = bf16[144,128]{1,0:T(8,128)(2,1)S(1)} collective-permute-done((bf16[144,128]{1,0:T(8,128)(2,1)S(1)}, bf16[144,128]{1,0:T(8,128)(2,1)S(1)}, u32[]{:S(2)}, u32[]{:S(2)}) %collective-permute-start.7) | collective-permute-done | bytes 36896 | tf_op jit(solution)/shard_map/ppermute | solution.py:332
  25.0 0.3 collective-permute-start.8
  25.2 1.1 %collective-permute-done.8.refs_1_ = f32[136,128]{1,0:T(8,128)S(1)} collective-permute-done((f32[136,128]{1,0:T(8,128)S(1)}, f32[136,128]{1,0:T(8,128)S(1)}, u32[]{:S(2)}, u32[]{:S(2)}) %collective-permute-start.8) | collective-permute-done | bytes 69664 | tf_op jit(solution)/shard_map/ppermute | solution.py:322
  26.3 0.8 %finish.1 = (f32[256,128]{1,0:T(8,128)}, f32[1,128]{1,0:T(1,128)}) custom-call(f32[136,128]{1,0:T(8,128)S(1)} %last_sum.1.refs_0_, f32[136,128]{1,0:T(8,128)S(1)} %collective-permute-done.8.refs_1_), custom_call_target="tpu_custom_call" | custom-call | flops 1000000000 | bytes 65536 | tf_op jit(solution)/shard_map/finish/pallas_call | solution.py:459
  (5 shorter events, 0.1 us)
Async XLA Ops:
  0.6 4.5 %copy-start = (bf16[1,8,5,128,128]{4,3,2,1,0:T(8,128)(2,1)S(1)}, bf16[1,8,5,128,128]{4,3,2,1,0:T(8,128)(2,1)}, u32[]{:S(2)}) copy-start(bf16[1,8,5,128,128]{4,3,2,1,0:T(8,128)(2,1)} %refs_2_.5) | copy-start | bytes 3932164
  0.6 1.1 %copy-start.1 = (bf16[1,1024,128]{2,1,0:T(8,128)(2,1)S(1)}, bf16[1,1024,128]{2,1,0:T(8,128)(2,1)}, u32[]{:S(2)}) copy-start(bf16[1,1024,128]{2,1,0:T(8,128)(2,1)} %refs_2_.3) | copy-start | bytes 786436
  1.7 3.4 %copy-start.2 = (bf16[1,1024,128]{2,1,0:T(8,128)(2,1)S(1)}, bf16[1,1024,128]{2,1,0:T(8,128)(2,1)}, u32[]{:S(2)}) copy-start(bf16[1,1024,128]{2,1,0:T(8,128)(2,1)} %refs_8_.1) | copy-start | bytes 786436
  1.7 3.4 %copy-start.3 = (bf16[256,128]{1,0:T(8,128)(2,1)S(1)}, bf16[256,128]{1,0:T(8,128)(2,1)}, u32[]{:S(2)}) copy-start(bf16[256,128]{1,0:T(8,128)(2,1)} %refs_3_.3) | copy-start | bytes 196612
  1.7 3.4 %copy-start.4 = (s32[1,8,5,128]{3,1,2,0:T(8,128)S(1)}, s32[1,8,5,128]{3,1,2,0:T(8,128)}, u32[]{:S(2)}) copy-start(s32[1,8,5,128]{3,1,2,0:T(8,128)} %param.12) | copy-start | bytes 61444
  1.7 3.4 %copy-start.5 = (s32[1,8,5]{1,0,2:T(1,128)S(1)}, s32[1,8,5]{1,0,2:T(1,128)}, u32[]{:S(2)}) copy-start(s32[1,8,5]{1,0,2:T(1,128)} %param.10) | copy-start | bytes 484
  1.7 3.4 %copy-start.6 = (f32[128]{0:T(128)S(1)}, f32[128]{0:T(128)}, u32[]{:S(2)}) copy-start(f32[128]{0:T(128)} %param.14) | copy-start | bytes 1540
  1.7 3.4 %copy-start.7 = (s32[1,8]{1,0:T(1,128)S(1)}, s32[1,8]{1,0:T(1,128)}, u32[]{:S(2)}) copy-start(s32[1,8]{1,0:T(1,128)} %refs_1_.5) | copy-start | bytes 100
  1.9 3.2 %collective-permute-start = (bf16[256,128]{1,0:T(8,128)(2,1)S(1)}, bf16[256,128]{1,0:T(8,128)(2,1)S(1)}, u32[]{:S(2)}, u32[]{:S(2)}) collective-permute-start(bf16[256,128]{1,0:T(8,128)(2,1)S(1)} %get-tuple-element.29), channel_id=1, source_target_pairs={{0,4},{4,0},{8,12},{12,8},{16,20},{20,16},{24,28},{28,24},{1,5},{5... | collective-permute-start | bytes 196616 | tf_op jit(solution)/shard_map/ppermute | solution.py:322
  2.5 4.9 %collective-permute-start.1 = (bf16[256,128]{1,0:T(8,128)(2,1)S(1)}, bf16[256,128]{1,0:T(8,128)(2,1)S(1)}, u32[]{:S(2)}, u32[]{:S(2)}) collective-permute-start(bf16[256,128]{1,0:T(8,128)(2,1)S(1)} %get-tuple-element.31), channel_id=1, source_target_pairs={{0,1},{1,0},{2,3},{3,2},{4,8},{5,9},{6,10},{7,11},{8,4},{9,5},{10,... | collective-permute-start | bytes 196616 | tf_op jit(solution)/shard_map/ppermute | solution.py:345
  7.9 1.4 %collective-permute-start.2 = (bf16[400,128]{1,0:T(8,128)(2,1)S(1)}, bf16[400,128]{1,0:T(8,128)(2,1)S(1)}, u32[]{:S(2)}, u32[]{:S(2)}) collective-permute-start(bf16[400,128]{1,0:T(8,128)(2,1)S(1)} %get-tuple-element.44), channel_id=1, source_target_pairs={{0,4},{4,0},{8,12},{12,8},{16,20},{20,16},{24,28},{28,24},{1,5},{5... | collective-permute-start | bytes 307208 | tf_op jit(solution)/shard_map/ppermute | solution.py:322
  9.3 4.2 %collective-permute-start.3 = (bf16[144,128]{1,0:T(8,128)(2,1)S(1)}, bf16[144,128]{1,0:T(8,128)(2,1)S(1)}, u32[]{:S(2)}, u32[]{:S(2)}) collective-permute-start(bf16[144,128]{1,0:T(8,128)(2,1)S(1)} %get-tuple-element.45.refs_0_), channel_id=1, source_target_pairs={{0,12},{1,4},{2,7},{3,15},{4,1},{5,9},{6,10},{7,2},{8,13},{9,5},{1... | collective-permute-start | bytes 110600 | tf_op jit(solution)/shard_map/ppermute | solution.py:332
  11.8 11.5 %collective-permute-start.5 = (bf16[256,128]{1,0:T(8,128)(2,1)S(1)}, bf16[256,128]{1,0:T(8,128)(2,1)S(1)}, u32[]{:S(2)}, u32[]{:S(2)}) collective-permute-start(bf16[256,128]{1,0:T(8,128)(2,1)S(1)} %get-tuple-element.46), channel_id=1, source_target_pairs={{0,1},{1,0},{2,3},{3,2},{4,8},{5,9},{6,10},{7,11},{8,4},{9,5},{10,... | collective-permute-start | bytes 196616 | tf_op jit(solution)/shard_map/ppermute | solution.py:345
  13.5 3.4 %collective-permute-start.4 = (bf16[144,128]{1,0:T(8,128)(2,1)S(1)}, bf16[144,128]{1,0:T(8,128)(2,1)S(1)}, u32[]{:S(2)}, u32[]{:S(2)}) collective-permute-start(bf16[144,128]{1,0:T(8,128)(2,1)S(1)} %next_sum.3.refs_7_.refs_0_), channel_id=1, source_target_pairs={{0,20},{1,7},{2,4},{3,23},{4,2},{5,17},{6,18},{7,1},{8,14},{9,29},... | collective-permute-start | bytes 110600 | tf_op jit(solution)/shard_map/ppermute | solution.py:332
  17.0 3.5 %collective-permute-start.6 = (bf16[144,128]{1,0:T(8,128)(2,1)S(1)}, bf16[144,128]{1,0:T(8,128)(2,1)S(1)}, u32[]{:S(2)}, u32[]{:S(2)}) collective-permute-start(bf16[144,128]{1,0:T(8,128)(2,1)S(1)} %next_sum.4.refs_8_.refs_0_), channel_id=1, source_target_pairs={{0,5},{1,13},{2,14},{3,6},{4,8},{5,0},{6,3},{7,11},{8,4},{9,12},{1... | collective-permute-start | bytes 110600 | tf_op jit(solution)/shard_map/ppermute | solution.py:332
  20.5 4.5 %collective-permute-start.7 = (bf16[144,128]{1,0:T(8,128)(2,1)S(1)}, bf16[144,128]{1,0:T(8,128)(2,1)S(1)}, u32[]{:S(2)}, u32[]{:S(2)}) collective-permute-start(bf16[144,128]{1,0:T(8,128)(2,1)S(1)} %next_sum.5.refs_5_.refs_0_), channel_id=1, source_target_pairs={{0,6},{1,21},{2,22},{3,5},{4,16},{5,3},{6,0},{7,19},{8,28},{9,15},... | collective-permute-start | bytes 110600 | tf_op jit(solution)/shard_map/ppermute | solution.py:332
  25.0 1.3 %collective-permute-start.8 = (f32[136,128]{1,0:T(8,128)S(1)}, f32[136,128]{1,0:T(8,128)S(1)}, u32[]{:S(2)}, u32[]{:S(2)}) collective-permute-start(f32[136,128]{1,0:T(8,128)S(1)} %last_sum.1.refs_0_), channel_id=1, source_target_pairs={{0,4},{4,0},{8,12},{12,8},{16,20},{20,16},{24,28},{28,24},{1,5},{5... | collective-permute-start | bytes 208904 | tf_op jit(solution)/shard_map/ppermute | solution.py:322

commit v3 on v2

--- a/solution.py
+++ b/solution.py
@@ -14,7 +14,6 @@
 BF16 = jnp.bfloat16
 VMEM = pl.BlockSpec(memory_space=pltpu.VMEM)
 ANY = pl.BlockSpec(memory_space=pl.ANY)
-HBM = pl.BlockSpec(memory_space=pltpu.HBM)
 SMEM = pl.BlockSpec(memory_space=pltpu.SMEM)
 
 
@@ -86,17 +85,10 @@
     return jnp.where((s < live[0, p]) & (q >= 0) & (q < panels), q, panels)
 
 
-def pick_halo(feat, far_rows, mate_rows, sems):
-    nodes, span = feat.shape[1], far_rows.shape[0]
+def pick_halo(low, high, far_rows, mate_rows):
     par = lax.axis_index("cluster") % 2
-    starts = ((nodes - span) * par, (nodes - span) * (1 - par))
-    copies = []
-    for i, (start, rows) in enumerate(zip(starts, (far_rows, mate_rows))):
-        source = feat.at[0, pl.ds(pl.multiple_of(start, span), span), :]
-        copies.append(pltpu.make_async_copy(source, rows, sems.at[i]))
-        copies[-1].start()
-    for copy in copies:
-        copy.wait()
+    far_rows[...] = jnp.where(par == 0, low[...], high[...])
+    mate_rows[...] = jnp.where(par == 0, high[...], low[...])
 
 
 def forward_near(
@@ -241,42 +233,37 @@
     grad_bias[...] = jnp.where(half == 0, mine[rows : rows + 1, :], got[rows : rows + 1, :]) * scale
 
 
-def spread(cols, live, tiles, weight, parts, recip, total, panel_list, first_row):
+def spread(cols, live, tiles, weight, turned, recip, total, panel_list, first_row):
     panels, slots, block = tiles.shape[1], tiles.shape[2], tiles.shape[3]
     width = weight.shape[1]
     first = lax.axis_index("cluster") * panels
+    both = dot(weight[...], turned)
     for j, p in enumerate(panel_list):
+        here = slice(j * block, (j + 1) * block)
+        total[p] = total[p] + both[:width, here]
         row = recip[first_row + j : first_row + j + 1, :]
-        scaled = (dot(weight[width:, :], parts[j]) * row).astype(BF16)
+        scaled = (both[width:, here] * row).astype(BF16)
         terms = dot(scaled, jnp.concatenate([tiles[0, p, s] for s in range(slots)], axis=1))
         for s in range(slots):
             q = own_slot(cols, live, p, s, first, panels)
             total[q] = total[q] + terms[:, s * block : (s + 1) * block]
 
 
-def backward_mid(cols, live, tiles, weight, near_t, far_t, recip, total):
+def backward_mid(cols, live, tiles, weight, near_t, recip, total):
     panels, block = tiles.shape[1], tiles.shape[3]
-    width = weight.shape[1]
-    edge, far, _ = edges(panels)
     mid = panels - 2 * REACH
-    parts = [near_t[:, j * block : (j + 1) * block] for j in range(mid + REACH)]
-    parts += [far_t[:, j * block : (j + 1) * block] for j in range(REACH)]
-    order = [REACH + j for j in range(mid)] + [edge + j for j in range(REACH)] + [far + j for j in range(REACH)]
-    for j, p in enumerate(order):
-        total[p] = dot(weight[:width, :], parts[j])
-    total[panels] = jnp.zeros((width, block), F32)
-    spread(cols, live, tiles, weight, parts, recip, total, order[:mid], 0)
+    total[...] = jnp.zeros(total.shape, F32)
+    spread(cols, live, tiles, weight, near_t[:, : mid * block], recip, total, [REACH + j for j in range(mid)], 0)
 
 
 def backward_rim(cols, live, tiles, weight, near_t, far_t, recip, before, total):
     panels, block = tiles.shape[1], tiles.shape[3]
+    mid = panels - 2 * REACH
     edge, far, _ = edges(panels)
-    mid = panels - 2 * REACH
-    parts = [near_t[:, j * block : (j + 1) * block] for j in range(mid, mid + REACH)]
-    parts += [far_t[:, j * block : (j + 1) * block] for j in range(REACH)]
     total[...] = before[...]
     order = [edge + j for j in range(REACH)] + [far + j for j in range(REACH)]
-    spread(cols, live, tiles, weight, parts, recip, total, order, mid)
+    turned = jnp.concatenate([near_t[:, mid * block :], far_t[...]], axis=1)
+    spread(cols, live, tiles, weight, turned, recip, total, order, panels - 2 * REACH)
 
 
 def gather_outputs(total, from_mate, from_far, out_near, out_far, grad, output, token):
@@ -362,10 +349,9 @@
         pick_halo,
         "pick_halo",
         [shape((span, width), BF16)] * 2,
-        [HBM],
-        [pltpu.SemaphoreType.DMA((2,))],
+        [VMEM] * 2,
         micros=8.0,
-    )(features)
+    )(features[0, :span], features[0, nodes - span :])
     mate_halo = swap_chip(mate_rows)
     far_halo = swap_far(far_rows)
     (out_near, near_t, recip, t_far, s_far, r_far, p_far, c_far, f_far, w_part, b_part, mate_ret) = call(
@@ -416,8 +402,8 @@
 
     def sum_mid(mine):
         made["total"] = call(
-            backward_mid, "backward_mid", shape((panels + 1, width, block), F32), [SMEM] * 2 + [VMEM] * 5, micros=1.2, after=1
-        )(columns, live_blocks, tiles, weight, near_t, far_t, recip, mine)
+            backward_mid, "backward_mid", shape((panels + 1, width, block), F32), [SMEM] * 2 + [VMEM] * 4, micros=1.2, after=1
+        )(columns, live_blocks, tiles, weight, near_t, recip, mine)
         return (made["total"],)
 
     def sum_rim(mine):

time: 27.2 us -> 26.9 us (0.989)
  Pallas kernels: 7.73 us -> 6.86 us
  waiting for transfers between devices: 5.38 us -> 6.07 us
    unnamed x16, local copies, waits for them, and re-layouts: 1.07 us -> 0.05 us
    squeeze x0 -> x1, local copies, waits for them, and re-layouts: none -> 0.89 us  [body(): features[0, nodes - span:]]
    ppermute x4, waiting for transfers between devices: 3.01 us -> 3.73 us  [swap_flips(): return lax.ppermute(block, ('cluster', 'batch'), pairs)]
    pallas_call x1, Pallas kernels: 1.5 us -> 1.1 us  [sum_mid(): call(backward_mid, 'backward_mid', shape((panels + 1, width, block), F32)...]
    pallas_call x1, Pallas kernels: 1.41 us -> 1.11 us  [sum_rim(): call(backward_rim, 'backward_rim', shape((panels + 1, width, block), F32)...]
  transfers between devices with their start and end apart: 9 -> 9, of which waited for: 7 -> 7; matrix products, arithmetic and copies ran while one was open for 0% -> 0% of each run, Pallas kernels for 23% -> 20%
where the time goes in v3:
time: 26.9 us; the launch traced here: 26.8 us
  starting transfers between devices  12.1 us (45%)
  Pallas kernels  6.86 us (26%)
  waiting for transfers between devices  6.07 us (23%)
  local copies, waits for them, and re-layouts  0.94 us (3%)
  between operations  0.8 us (3%)
    ppermute x4, starting transfers between devices, swap_flips(): return lax.ppermute(block, ('cluster', 'batch'), pairs)  8.58 us
    ppermute x4, waiting for transfers between devices, swap_flips(): return lax.ppermute(block, ('cluster', 'batch'), pairs)  3.73 us
    ppermute x2, starting transfers between devices, swap_far(): return lax.ppermute(block, ('cluster', 'batch'), pairs)  2.65 us
    ppermute x3, waiting for transfers between devices, swap_chip(): return lax.ppermute(block, 'cluster', [(c, c ^ 1) for c in range(nc)])  2.05 us
    pallas_call x1, Pallas kernels, body(): call(forward_near, 'forward_near', [shape((near, hidden), BF16), shape((h...  1.88 us
    pallas_call x1, Pallas kernels, sum_rim(): call(backward_rim, 'backward_rim', shape((panels + 1, width, block), F32)...  1.11 us
    pallas_call x1, Pallas kernels, sum_mid(): call(backward_mid, 'backward_mid', shape((panels + 1, width, block), F32)...  1.1 us
    pallas_call x1, Pallas kernels, write_outputs(): call(gather_outputs, 'gather_outputs', [shape((1, nodes, width), F32), sh...  1.02 us
  transfers between devices with their start and end apart: 9, of which 7 were waited for; matrix products, arithmetic and copies ran while one was open for 0% of the time, Pallas kernels for 20%

profile of v3, /device:TPU:0, one launch (start us, length us, event | category | flops | bytes accessed | tf_op | source)
XLA Modules:
  0.0 26.8 jit_solution(8106346583178921846)
XLA Ops:
  0.6 0.9 %slice_bitcast_fusion = (bf16[256,128]{1,0:T(8,128)(2,1)S(1)}, bf16[256,128]{1,0:T(8,128)(2,1)S(1)}) fusion(bf16[1,1024,128]{2,1,0:T(8,128)(2,1)} %refs_2_.3), kind=kLoop, calls=%fused_computation | loop fusion | bytes 262144 | tf_op jit(solution)/shard_map/squeeze | solution.py:354
  1.5 0.0 copy-start
  1.5 0.0 copy-start.1
  1.5 0.0 copy-start.2
  1.6 0.0 copy-start.3
  1.6 0.0 copy-start.4
  1.6 0.0 copy-start.5
  1.6 0.0 copy-start.6
  1.6 0.0 copy-start.7
  1.7 0.5 %collective-permute-start = (bf16[256,128]{1,0:T(8,128)(2,1)S(1)}, bf16[256,128]{1,0:T(8,128)(2,1)S(1)}, u32[]{:S(2)}, u32[]{:S(2)}) collective-permute-start(bf16[256,128]{1,0:T(8,128)(2,1)S(1)} %get-tuple-element.29), channel_id=1, source_target_pairs={{0,4},{4,0},{8,12},{12,8},{16,20},{20,16},{24,28},{28,24},{1,5},{5... | collective-permute-start | bytes 196616 | tf_op jit(solution)/shard_map/ppermute | solution.py:309
  2.2 2.6 %collective-permute-start.1 = (bf16[256,128]{1,0:T(8,128)(2,1)S(1)}, bf16[256,128]{1,0:T(8,128)(2,1)S(1)}, u32[]{:S(2)}, u32[]{:S(2)}) collective-permute-start(bf16[256,128]{1,0:T(8,128)(2,1)S(1)} %get-tuple-element.31), channel_id=1, source_target_pairs={{0,1},{1,0},{2,3},{3,2},{4,8},{5,9},{6,10},{7,11},{8,4},{9,5},{10,... | collective-permute-start | bytes 196616 | tf_op jit(solution)/shard_map/ppermute | solution.py:332
  4.8 0.0 collective-permute-done.refs_3_
  4.8 0.0 copy-done
  4.8 0.0 copy-done.1
  4.8 0.0 copy-done.2
  4.8 0.0 copy-done.3
  4.9 0.0 copy-done.4
  4.9 0.0 copy-done.5
  4.9 0.0 copy-done.6
  4.9 0.0 copy-done.7
  4.9 1.9 %forward_near.1 = (bf16[768,128]{1,0:T(8,128)(2,1)S(1)}, bf16[128,768]{1,0:T(8,128)(2,1)S(1)}, f32[8,128]{1,0:T(8,128)S(1)}, bf16[256,256]{1,0:T(8,128)(2,1)S(1)...) custom-call(s32[5,1,8]{2,1,0:T(1,128)S(1)} %bitcast.9, ...), custom_call_target="tpu_custom_call" | custom-call | flops 2000000000 | bytes 65536 | tf_op jit(solution)/shard_map/forward_near/pallas_call | solution.py:357
  6.8 0.3 %collective-permute-done.1.refs_0_ = bf16[256,128]{1,0:T(8,128)(2,1)S(1)} collective-permute-done((bf16[256,128]{1,0:T(8,128)(2,1)S(1)}, bf16[256,128]{1,0:T(8,128)(2,1)S(1)}, u32[]{:S(2)}, u32[]{:S(2)}) %collective-permute-start.1) | collective-permute-done | bytes 65568 | tf_op jit(solution)/shard_map/ppermute | solution.py:332
  7.1 0.5 %forward_far.1 = (bf16[256,128]{1,0:T(8,128)(2,1)S(1)}, bf16[128,256]{1,0:T(8,128)(2,1)S(1)}, f32[144,128]{1,0:T(8,128)S(1)}, bf16[400,128]{1,0:T(8,128)(2,1)S(1)}) custom-call(bf16[256,128]{1,0:T(8,128)(2,1)S(1)} %collective-permute-done.1.refs_0_, bf16[256,256]{1,0:T(8,128)(2,1)S(1)} %get-tuple-element.32.refs_1_.refs_2_, ...), custom_call_target="tpu_custom_call" | custom-call | flops 1000000000 | bytes 65536 | tf_op jit(solution)/shard_map/forward_far/pallas_call | solution.py:378
  7.6 0.1 collective-permute-start.2
  7.7 0.3 %return_far.1.refs_2_ = bf16[256,128]{1,0:T(8,128)(2,1)S(1)} custom-call(bf16[256,128]{1,0:T(8,128)(2,1)S(1)} %copy-done.3, bf16[128,256]{1,0:T(8,128)(2,1)S(1)} %get-tuple-element.41.refs_1_.refs_5_, bf16[256,256]{1,0:T(8,128)(2,1)S(1)} %get-tuple-element.32.refs_1_.refs_2_, f32[8,128]{1,0:T(8,128)S(1)} %get-tuple-element.42.refs_3_.refs_5_.refs_6_), custom_call_target="tpu_custom_call" | custom-call | flops 300000000 | bytes 65536 | tf_op jit(solution)/shard_map/return_far/pallas_call | solution.py:391
  8.0 1.0 %collective-permute-done.2.refs_1_ = bf16[400,128]{1,0:T(8,128)(2,1)S(1)} collective-permute-done((bf16[400,128]{1,0:T(8,128)(2,1)S(1)}, bf16[400,128]{1,0:T(8,128)(2,1)S(1)}, u32[]{:S(2)}, u32[]{:S(2)}) %collective-permute-start.2) | collective-permute-done | bytes 102432 | tf_op jit(solution)/shard_map/ppermute | solution.py:309
  9.0 2.5 %collective-permute-start.3 = (bf16[144,128]{1,0:T(8,128)(2,1)S(1)}, bf16[144,128]{1,0:T(8,128)(2,1)S(1)}, u32[]{:S(2)}, u32[]{:S(2)}) collective-permute-start(bf16[144,128]{1,0:T(8,128)(2,1)S(1)} %get-tuple-element.45.refs_0_), channel_id=1, source_target_pairs={{0,12},{1,4},{2,7},{3,15},{4,1},{5,9},{6,10},{7,2},{8,13},{9,5},{1... | collective-permute-start | bytes 110600 | tf_op jit(solution)/shard_map/ppermute | solution.py:319
  11.5 0.0 collective-permute-start.5
  11.5 1.6 %collective-permute-done.3.refs_1_ = bf16[144,128]{1,0:T(8,128)(2,1)S(1)} collective-permute-done((bf16[144,128]{1,0:T(8,128)(2,1)S(1)}, bf16[144,128]{1,0:T(8,128)(2,1)S(1)}, u32[]{:S(2)}, u32[]{:S(2)}) %collective-permute-start.3) | collective-permute-done | bytes 36896 | tf_op jit(solution)/shard_map/ppermute | solution.py:319
  13.2 1.4 %collective-permute-start.4 = (bf16[144,128]{1,0:T(8,128)(2,1)S(1)}, bf16[144,128]{1,0:T(8,128)(2,1)S(1)}, u32[]{:S(2)}, u32[]{:S(2)}) collective-permute-start(bf16[144,128]{1,0:T(8,128)(2,1)S(1)} %next_sum.3.refs_6_.refs_0_), channel_id=1, source_target_pairs={{0,20},{1,7},{2,4},{3,23},{4,2},{5,17},{6,18},{7,1},{8,14},{9,29},... | collective-permute-start | bytes 110600 | tf_op jit(solution)/shard_map/ppermute | solution.py:319
  14.6 1.1 %backward_mid.1.refs_2_.refs_7_ = f32[9,128,128]{2,1,0:T(8,128)S(1)} custom-call(s32[5,1,8]{2,1,0:T(1,128)S(1)} %bitcast.10, s32[1,8]{1,0:T(1,128)S(1)} %copy-done.7, bf16[1,8,5,128,128]{4,3,2,1,0:T(8,128)(2,1)S(1)} %copy-done.1, bf16[256,128]{1,0:T(8,128)(2,1)S(1)} %copy-done.3, bf16[128,768]{1,0:T(8,128)(2,1)S(1)} %get-tuple-element.30.refs_4_, ...), custom_call_target="tpu_custom_call" | custom-call | flops 1200000000 | bytes 65536 | tf_op jit(solution)/shard_map/backward_mid/pallas_call | solution.py:404
  15.7 0.9 %collective-permute-done.4.refs_1_ = bf16[144,128]{1,0:T(8,128)(2,1)S(1)} collective-permute-done((bf16[144,128]{1,0:T(8,128)(2,1)S(1)}, bf16[144,128]{1,0:T(8,128)(2,1)S(1)}, u32[]{:S(2)}, u32[]{:S(2)}) %collective-permute-start.4) | collective-permute-done | bytes 36896 | tf_op jit(solution)/shard_map/ppermute | solution.py:319
  16.7 1.9 %collective-permute-start.6 = (bf16[144,128]{1,0:T(8,128)(2,1)S(1)}, bf16[144,128]{1,0:T(8,128)(2,1)S(1)}, u32[]{:S(2)}, u32[]{:S(2)}) collective-permute-start(bf16[144,128]{1,0:T(8,128)(2,1)S(1)} %next_sum.4.refs_8_.refs_0_), channel_id=1, source_target_pairs={{0,5},{1,13},{2,14},{3,6},{4,8},{5,0},{6,3},{7,11},{8,4},{9,12},{1... | collective-permute-start | bytes 110600 | tf_op jit(solution)/shard_map/ppermute | solution.py:319
  18.5 1.1 %backward_rim.1.refs_2_.refs_0_ = f32[9,128,128]{2,1,0:T(8,128)S(1)} custom-call(s32[5,1,8]{2,1,0:T(1,128)S(1)} %bitcast.11, s32[1,8]{1,0:T(1,128)S(1)} %copy-done.7, bf16[1,8,5,128,128]{4,3,2,1,0:T(8,128)(2,1)S(1)} %copy-done.1, bf16[256,128]{1,0:T(8,128)(2,1)S(1)} %copy-done.3, bf16[128,768]{1,0:T(8,128)(2,1)S(1)} %get-tuple-element.30.refs_4_, ...), custom_call_target="tpu_custom_call" | custom-call | flops 1200000000 | bytes 65536 | tf_op jit(solution)/shard_map/backward_rim/pallas_call | solution.py:410
  19.6 0.5 %collective-permute-done.6.refs_1_ = bf16[144,128]{1,0:T(8,128)(2,1)S(1)} collective-permute-done((bf16[144,128]{1,0:T(8,128)(2,1)S(1)}, bf16[144,128]{1,0:T(8,128)(2,1)S(1)}, u32[]{:S(2)}, u32[]{:S(2)}) %collective-permute-start.6) | collective-permute-done | bytes 36896 | tf_op jit(solution)/shard_map/ppermute | solution.py:319
  20.2 2.8 %collective-permute-start.7 = (bf16[144,128]{1,0:T(8,128)(2,1)S(1)}, bf16[144,128]{1,0:T(8,128)(2,1)S(1)}, u32[]{:S(2)}, u32[]{:S(2)}) collective-permute-start(bf16[144,128]{1,0:T(8,128)(2,1)S(1)} %next_sum.5.refs_5_.refs_0_), channel_id=1, source_target_pairs={{0,6},{1,21},{2,22},{3,5},{4,16},{5,3},{6,0},{7,19},{8,28},{9,15},... | collective-permute-start | bytes 110600 | tf_op jit(solution)/shard_map/ppermute | solution.py:319
  23.0 0.0 collective-permute-done.5.refs_2_
  23.0 1.0 %gather_outputs.1 = (f32[1,1024,128]{2,1,0:T(8,128)}, bf16[1,1024,128]{2,1,0:T(8,128)(2,1)}, f32[8,128]{1,0:T(8,128)S(1)}) custom-call(f32[9,128,128]{2,1,0:T(8,128)S(1)} %backward_rim.1.refs_2_.refs_0_, bf16[400,128]{1,0:T(8,128)(2,1)S(1)} %collective-permute-done.2.refs_1_, bf16[256,128]{1,0:T(8,128)(2,1)S(1)} %collective-permute-done.5.refs_2_, ...), custom_call_target="tpu_custom_call" | custom-call | flops 1000000000 | bytes 65536 | tf_op jit(solution)/shard_map/gather_outputs/pallas_call | solution.py:416
  24.0 0.6 %collective-permute-done.7.refs_1_ = bf16[144,128]{1,0:T(8,128)(2,1)S(1)} collective-permute-done((bf16[144,128]{1,0:T(8,128)(2,1)S(1)}, bf16[144,128]{1,0:T(8,128)(2,1)S(1)}, u32[]{:S(2)}, u32[]{:S(2)}) %collective-permute-start.7) | collective-permute-done | bytes 36896 | tf_op jit(solution)/shard_map/ppermute | solution.py:319
  24.7 0.3 collective-permute-start.8
  24.9 1.1 %collective-permute-done.8.refs_1_ = f32[136,128]{1,0:T(8,128)S(1)} collective-permute-done((f32[136,128]{1,0:T(8,128)S(1)}, f32[136,128]{1,0:T(8,128)S(1)}, u32[]{:S(2)}, u32[]{:S(2)}) %collective-permute-start.8) | collective-permute-done | bytes 69664 | tf_op jit(solution)/shard_map/ppermute | solution.py:309
  26.0 0.8 %finish.1 = (f32[256,128]{1,0:T(8,128)}, f32[1,128]{1,0:T(1,128)}) custom-call(f32[136,128]{1,0:T(8,128)S(1)} %last_sum.1.refs_0_, f32[136,128]{1,0:T(8,128)S(1)} %collective-permute-done.8.refs_1_), custom_call_target="tpu_custom_call" | custom-call | flops 1000000000 | bytes 65536 | tf_op jit(solution)/shard_map/finish/pallas_call | solution.py:445
  (6 shorter events, 0.2 us)
Async XLA Ops:
  1.5 3.3 %copy-start = (bf16[1,1024,128]{2,1,0:T(8,128)(2,1)S(1)}, bf16[1,1024,128]{2,1,0:T(8,128)(2,1)}, u32[]{:S(2)}) copy-start(bf16[1,1024,128]{2,1,0:T(8,128)(2,1)} %refs_2_.3) | copy-start | bytes 786436
  1.5 3.3 %copy-start.1 = (bf16[1,8,5,128,128]{4,3,2,1,0:T(8,128)(2,1)S(1)}, bf16[1,8,5,128,128]{4,3,2,1,0:T(8,128)(2,1)}, u32[]{:S(2)}) copy-start(bf16[1,8,5,128,128]{4,3,2,1,0:T(8,128)(2,1)} %refs_2_.5) | copy-start | bytes 3932164
  1.5 3.3 %copy-start.2 = (bf16[1,1024,128]{2,1,0:T(8,128)(2,1)S(1)}, bf16[1,1024,128]{2,1,0:T(8,128)(2,1)}, u32[]{:S(2)}) copy-start(bf16[1,1024,128]{2,1,0:T(8,128)(2,1)} %refs_8_.1) | copy-start | bytes 786436
  1.6 3.3 %copy-start.3 = (bf16[256,128]{1,0:T(8,128)(2,1)S(1)}, bf16[256,128]{1,0:T(8,128)(2,1)}, u32[]{:S(2)}) copy-start(bf16[256,128]{1,0:T(8,128)(2,1)} %refs_3_.3) | copy-start | bytes 196612
  1.6 3.3 %copy-start.4 = (s32[1,8,5,128]{3,1,2,0:T(8,128)S(1)}, s32[1,8,5,128]{3,1,2,0:T(8,128)}, u32[]{:S(2)}) copy-start(s32[1,8,5,128]{3,1,2,0:T(8,128)} %param.12) | copy-start | bytes 61444
  1.6 3.3 %copy-start.5 = (s32[1,8,5]{1,0,2:T(1,128)S(1)}, s32[1,8,5]{1,0,2:T(1,128)}, u32[]{:S(2)}) copy-start(s32[1,8,5]{1,0,2:T(1,128)} %param.10) | copy-start | bytes 484
  1.6 3.3 %copy-start.6 = (f32[128]{0:T(128)S(1)}, f32[128]{0:T(128)}, u32[]{:S(2)}) copy-start(f32[128]{0:T(128)} %param.14) | copy-start | bytes 1540
  1.6 3.3 %copy-start.7 = (s32[1,8]{1,0:T(1,128)S(1)}, s32[1,8]{1,0:T(1,128)}, u32[]{:S(2)}) copy-start(s32[1,8]{1,0:T(1,128)} %refs_1_.5) | copy-start | bytes 100
  1.7 3.2 %collective-permute-start = (bf16[256,128]{1,0:T(8,128)(2,1)S(1)}, bf16[256,128]{1,0:T(8,128)(2,1)S(1)}, u32[]{:S(2)}, u32[]{:S(2)}) collective-permute-start(bf16[256,128]{1,0:T(8,128)(2,1)S(1)} %get-tuple-element.29), channel_id=1, source_target_pairs={{0,4},{4,0},{8,12},{12,8},{16,20},{20,16},{24,28},{28,24},{1,5},{5... | collective-permute-start | bytes 196616 | tf_op jit(solution)/shard_map/ppermute | solution.py:309
  2.2 4.9 %collective-permute-start.1 = (bf16[256,128]{1,0:T(8,128)(2,1)S(1)}, bf16[256,128]{1,0:T(8,128)(2,1)S(1)}, u32[]{:S(2)}, u32[]{:S(2)}) collective-permute-start(bf16[256,128]{1,0:T(8,128)(2,1)S(1)} %get-tuple-element.31), channel_id=1, source_target_pairs={{0,1},{1,0},{2,3},{3,2},{4,8},{5,9},{6,10},{7,11},{8,4},{9,5},{10,... | collective-permute-start | bytes 196616 | tf_op jit(solution)/shard_map/ppermute | solution.py:332
  7.6 1.4 %collective-permute-start.2 = (bf16[400,128]{1,0:T(8,128)(2,1)S(1)}, bf16[400,128]{1,0:T(8,128)(2,1)S(1)}, u32[]{:S(2)}, u32[]{:S(2)}) collective-permute-start(bf16[400,128]{1,0:T(8,128)(2,1)S(1)} %get-tuple-element.44), channel_id=1, source_target_pairs={{0,4},{4,0},{8,12},{12,8},{16,20},{20,16},{24,28},{28,24},{1,5},{5... | collective-permute-start | bytes 307208 | tf_op jit(solution)/shard_map/ppermute | solution.py:309
  9.0 4.2 %collective-permute-start.3 = (bf16[144,128]{1,0:T(8,128)(2,1)S(1)}, bf16[144,128]{1,0:T(8,128)(2,1)S(1)}, u32[]{:S(2)}, u32[]{:S(2)}) collective-permute-start(bf16[144,128]{1,0:T(8,128)(2,1)S(1)} %get-tuple-element.45.refs_0_), channel_id=1, source_target_pairs={{0,12},{1,4},{2,7},{3,15},{4,1},{5,9},{6,10},{7,2},{8,13},{9,5},{1... | collective-permute-start | bytes 110600 | tf_op jit(solution)/shard_map/ppermute | solution.py:319
  11.5 11.5 %collective-permute-start.5 = (bf16[256,128]{1,0:T(8,128)(2,1)S(1)}, bf16[256,128]{1,0:T(8,128)(2,1)S(1)}, u32[]{:S(2)}, u32[]{:S(2)}) collective-permute-start(bf16[256,128]{1,0:T(8,128)(2,1)S(1)} %get-tuple-element.46), channel_id=1, source_target_pairs={{0,1},{1,0},{2,3},{3,2},{4,8},{5,9},{6,10},{7,11},{8,4},{9,5},{10,... | collective-permute-start | bytes 196616 | tf_op jit(solution)/shard_map/ppermute | solution.py:332
  13.2 3.4 %collective-permute-start.4 = (bf16[144,128]{1,0:T(8,128)(2,1)S(1)}, bf16[144,128]{1,0:T(8,128)(2,1)S(1)}, u32[]{:S(2)}, u32[]{:S(2)}) collective-permute-start(bf16[144,128]{1,0:T(8,128)(2,1)S(1)} %next_sum.3.refs_6_.refs_0_), channel_id=1, source_target_pairs={{0,20},{1,7},{2,4},{3,23},{4,2},{5,17},{6,18},{7,1},{8,14},{9,29},... | collective-permute-start | bytes 110600 | tf_op jit(solution)/shard_map/ppermute | solution.py:319
  16.7 3.5 %collective-permute-start.6 = (bf16[144,128]{1,0:T(8,128)(2,1)S(1)}, bf16[144,128]{1,0:T(8,128)(2,1)S(1)}, u32[]{:S(2)}, u32[]{:S(2)}) collective-permute-start(bf16[144,128]{1,0:T(8,128)(2,1)S(1)} %next_sum.4.refs_8_.refs_0_), channel_id=1, source_target_pairs={{0,5},{1,13},{2,14},{3,6},{4,8},{5,0},{6,3},{7,11},{8,4},{9,12},{1... | collective-permute-start | bytes 110600 | tf_op jit(solution)/shard_map/ppermute | solution.py:319
  20.2 4.5 %collective-permute-start.7 = (bf16[144,128]{1,0:T(8,128)(2,1)S(1)}, bf16[144,128]{1,0:T(8,128)(2,1)S(1)}, u32[]{:S(2)}, u32[]{:S(2)}) collective-permute-start(bf16[144,128]{1,0:T(8,128)(2,1)S(1)} %next_sum.5.refs_5_.refs_0_), channel_id=1, source_target_pairs={{0,6},{1,21},{2,22},{3,5},{4,16},{5,3},{6,0},{7,19},{8,28},{9,15},... | collective-permute-start | bytes 110600 | tf_op jit(solution)/shard_map/ppermute | solution.py:319
  24.7 1.3 %collective-permute-start.8 = (f32[136,128]{1,0:T(8,128)S(1)}, f32[136,128]{1,0:T(8,128)S(1)}, u32[]{:S(2)}, u32[]{:S(2)}) collective-permute-start(f32[136,128]{1,0:T(8,128)S(1)} %last_sum.1.refs_0_), channel_id=1, source_target_pairs={{0,4},{4,0},{8,12},{12,8},{16,20},{20,16},{24,28},{28,24},{1,5},{5... | collective-permute-start | bytes 208904 | tf_op jit(solution)/shard_map/ppermute | solution.py:309

commit v4 on v3

--- a/solution.py
+++ b/solution.py
@@ -150,7 +150,7 @@
     slope = (cot_near.astype(F32) * rise).astype(BF16)
     turned = slope.T
     slope_t[...] = turned
-    w_part[...] = dot(turned, joined)
+    w_part[...] = dot(turned, joined).T
     b_part[...] = jnp.broadcast_to(jnp.sum(slope.astype(F32), axis=0, keepdims=True), b_part.shape)
     scale_row = jnp.concatenate([recip_rows[mid + j : mid + j + 1] for j in range(REACH)], axis=1)
     scaled = (dot(weight[width:, :], turned[:, mid * block :]) * scale_row).astype(BF16)
@@ -182,9 +182,9 @@
     slope = (c_far[...].astype(F32) * rise).astype(BF16)
     turned = slope.T
     slope_t[...] = turned
-    total = w_part[...] + dot(turned, jnp.concatenate([f_far[...], mean], axis=1))
+    total = w_part[...] + dot(jnp.concatenate([f_far[...].T, mean.T], axis=0), slope)
     b_total = b_part[0:1, :] + jnp.sum(slope.astype(F32), axis=0, keepdims=True)
-    low, high = total[:, :width], total[:, width:]
+    low, high = total[:width], total[width:]
     rows = low.shape[0]
     kept[0:rows, :] = jnp.where(half == 0, low, high)
     kept[rows:, :] = jnp.broadcast_to(b_total, (kept.shape[0] - rows, width))
@@ -226,8 +226,8 @@
 def finish(mine, got, grad, grad_bias, *, clusters, batches, scale):
     half = half_of(clusters, batches)
     rows = grad.shape[0] // 2
-    own = mine[0:rows, :].T * scale
-    other = got[0:rows, :].T * scale
+    own = mine[0:rows, :].astype(F32) * scale
+    other = got[0:rows, :].astype(F32) * scale
     grad[0:rows, :] = jnp.where(half == 0, own, other)
     grad[rows:, :] = jnp.where(half == 0, other, own)
     grad_bias[...] = jnp.where(half == 0, mine[rows : rows + 1, :], got[rows : rows + 1, :]) * scale
@@ -339,7 +339,7 @@
     nc, nb = lax.axis_size("cluster"), lax.axis_size("batch")
     span = REACH * block
     near = nodes - span
-    rows = hidden + TAIL
+    rows = width + TAIL
     shape = jax.ShapeDtypeStruct
     sizes = dict(clusters=nc, batches=nb)
     columns = jnp.transpose(columns, (2, 0, 1))
@@ -367,7 +367,7 @@
             shape((span, hidden), F32),
             shape((span, hidden), BF16),
             shape((span, width), BF16),
-            shape((hidden, 2 * width), F32),
+            shape((2 * width, hidden), F32),
             shape((8, hidden), F32),
             shape((span, block), BF16),
         ],
@@ -381,8 +381,8 @@
         [
             shape((span, hidden), BF16),
             shape((hidden, span), BF16),
-            shape((rows, width), F32),
-            shape((rows + span, width), BF16),
+            shape((rows, hidden), F32),
+            shape((rows + span, hidden), BF16),
         ],
         [VMEM] * 11,
         **sizes,
@@ -436,7 +436,7 @@
             )
         else:
             mine = call(
-                last_sum, "last_sum", shape((hidden + 8, width), F32), [VMEM] * 2, micros=0.1, after=len(held)
+                last_sum, "last_sum", shape((width + 8, hidden), F32), [VMEM] * 2, micros=0.1, after=len(held)
             )(mine, other, *held)
     for task in tasks:
         task(mine)

time: 26.9 us -> 26.9 us (level)
  transfers between devices with their start and end apart: 9 -> 9, of which waited for: 7 -> 7; matrix products, arithmetic and copies ran while one was open for 0% -> 0% of each run, Pallas kernels for 20% -> 21%
where the time goes in v4:
time: 26.9 us; the launch traced here: 26.7 us
  starting transfers between devices  12.1 us (45%)
  Pallas kernels  6.78 us (25%)
  waiting for transfers between devices  6.07 us (23%)
  local copies, waits for them, and re-layouts  0.94 us (3%)
  between operations  0.8 us (3%)
    ppermute x4, starting transfers between devices, swap_flips(): return lax.ppermute(block, ('cluster', 'batch'), pairs)  8.58 us
    ppermute x4, waiting for transfers between devices, swap_flips(): return lax.ppermute(block, ('cluster', 'batch'), pairs)  3.73 us
    ppermute x2, starting transfers between devices, swap_far(): return lax.ppermute(block, ('cluster', 'batch'), pairs)  2.65 us
    ppermute x3, waiting for transfers between devices, swap_chip(): return lax.ppermute(block, 'cluster', [(c, c ^ 1) for c in range(nc)])  2.05 us
    pallas_call x1, Pallas kernels, body(): call(forward_near, 'forward_near', [shape((near, hidden), BF16), shape((h...  1.88 us
    pallas_call x1, Pallas kernels, sum_rim(): call(backward_rim, 'backward_rim', shape((panels + 1, width, block), F32)...  1.11 us
    pallas_call x1, Pallas kernels, sum_mid(): call(backward_mid, 'backward_mid', shape((panels + 1, width, block), F32)...  1.1 us
    pallas_call x1, Pallas kernels, write_outputs(): call(gather_outputs, 'gather_outputs', [shape((1, nodes, width), F32), sh...  1.02 us
  transfers between devices with their start and end apart: 9, of which 7 were waited for; matrix products, arithmetic and copies ran while one was open for 0% of the time, Pallas kernels for 21%

profile of v4, /device:TPU:0, one launch (start us, length us, event | category | flops | bytes accessed | tf_op | source)
XLA Modules:
  0.0 26.7 jit_solution(13543491990441060098)
XLA Ops:
  0.6 0.9 %slice_bitcast_fusion = (bf16[256,128]{1,0:T(8,128)(2,1)S(1)}, bf16[256,128]{1,0:T(8,128)(2,1)S(1)}) fusion(bf16[1,1024,128]{2,1,0:T(8,128)(2,1)} %refs_2_.3), kind=kLoop, calls=%fused_computation | loop fusion | bytes 262144 | tf_op jit(solution)/shard_map/squeeze | solution.py:354
  1.5 0.0 copy-start
  1.5 0.0 copy-start.1
  1.5 0.0 copy-start.2
  1.6 0.0 copy-start.3
  1.6 0.0 copy-start.4
  1.6 0.0 copy-start.5
  1.6 0.0 copy-start.6
  1.6 0.0 copy-start.7
  1.7 0.5 %collective-permute-start = (bf16[256,128]{1,0:T(8,128)(2,1)S(1)}, bf16[256,128]{1,0:T(8,128)(2,1)S(1)}, u32[]{:S(2)}, u32[]{:S(2)}) collective-permute-start(bf16[256,128]{1,0:T(8,128)(2,1)S(1)} %get-tuple-element.29), channel_id=1, source_target_pairs={{0,4},{4,0},{8,12},{12,8},{16,20},{20,16},{24,28},{28,24},{1,5},{5... | collective-permute-start | bytes 196616 | tf_op jit(solution)/shard_map/ppermute | solution.py:309
  2.2 2.6 %collective-permute-start.1 = (bf16[256,128]{1,0:T(8,128)(2,1)S(1)}, bf16[256,128]{1,0:T(8,128)(2,1)S(1)}, u32[]{:S(2)}, u32[]{:S(2)}) collective-permute-start(bf16[256,128]{1,0:T(8,128)(2,1)S(1)} %get-tuple-element.31), channel_id=1, source_target_pairs={{0,1},{1,0},{2,3},{3,2},{4,8},{5,9},{6,10},{7,11},{8,4},{9,5},{10,... | collective-permute-start | bytes 196616 | tf_op jit(solution)/shard_map/ppermute | solution.py:332
  4.8 0.0 collective-permute-done.refs_3_
  4.8 0.0 copy-done
  4.8 0.0 copy-done.1
  4.8 0.0 copy-done.2
  4.8 0.0 copy-done.3
  4.9 0.0 copy-done.4
  4.9 0.0 copy-done.5
  4.9 0.0 copy-done.6
  4.9 0.0 copy-done.7
  4.9 1.9 %forward_near.1 = (bf16[768,128]{1,0:T(8,128)(2,1)S(1)}, bf16[128,768]{1,0:T(8,128)(2,1)S(1)}, f32[8,128]{1,0:T(8,128)S(1)}, bf16[256,256]{1,0:T(8,128)(2,1)S(1)...) custom-call(s32[5,1,8]{2,1,0:T(1,128)S(1)} %bitcast.9, ...), custom_call_target="tpu_custom_call" | custom-call | flops 2000000000 | bytes 65536 | tf_op jit(solution)/shard_map/forward_near/pallas_call | solution.py:357
  6.8 0.3 %collective-permute-done.1.refs_0_ = bf16[256,128]{1,0:T(8,128)(2,1)S(1)} collective-permute-done((bf16[256,128]{1,0:T(8,128)(2,1)S(1)}, bf16[256,128]{1,0:T(8,128)(2,1)S(1)}, u32[]{:S(2)}, u32[]{:S(2)}) %collective-permute-start.1) | collective-permute-done | bytes 65568 | tf_op jit(solution)/shard_map/ppermute | solution.py:332
  7.1 0.5 %forward_far.1 = (bf16[256,128]{1,0:T(8,128)(2,1)S(1)}, bf16[128,256]{1,0:T(8,128)(2,1)S(1)}, f32[144,128]{1,0:T(8,128)S(1)}, bf16[400,128]{1,0:T(8,128)(2,1)S(1)}) custom-call(bf16[256,128]{1,0:T(8,128)(2,1)S(1)} %collective-permute-done.1.refs_0_, bf16[256,256]{1,0:T(8,128)(2,1)S(1)} %get-tuple-element.32.refs_1_.refs_2_, ...), custom_call_target="tpu_custom_call" | custom-call | flops 1000000000 | bytes 65536 | tf_op jit(solution)/shard_map/forward_far/pallas_call | solution.py:378
  7.6 0.1 collective-permute-start.2
  7.7 0.3 %return_far.1.refs_2_ = bf16[256,128]{1,0:T(8,128)(2,1)S(1)} custom-call(bf16[256,128]{1,0:T(8,128)(2,1)S(1)} %copy-done.3, bf16[128,256]{1,0:T(8,128)(2,1)S(1)} %get-tuple-element.41.refs_1_.refs_5_, bf16[256,256]{1,0:T(8,128)(2,1)S(1)} %get-tuple-element.32.refs_1_.refs_2_, f32[8,128]{1,0:T(8,128)S(1)} %get-tuple-element.42.refs_3_.refs_5_.refs_6_), custom_call_target="tpu_custom_call" | custom-call | flops 300000000 | bytes 65536 | tf_op jit(solution)/shard_map/return_far/pallas_call | solution.py:391
  8.0 1.0 %collective-permute-done.2.refs_1_ = bf16[400,128]{1,0:T(8,128)(2,1)S(1)} collective-permute-done((bf16[400,128]{1,0:T(8,128)(2,1)S(1)}, bf16[400,128]{1,0:T(8,128)(2,1)S(1)}, u32[]{:S(2)}, u32[]{:S(2)}) %collective-permute-start.2) | collective-permute-done | bytes 102432 | tf_op jit(solution)/shard_map/ppermute | solution.py:309
  9.0 2.5 %collective-permute-start.3 = (bf16[144,128]{1,0:T(8,128)(2,1)S(1)}, bf16[144,128]{1,0:T(8,128)(2,1)S(1)}, u32[]{:S(2)}, u32[]{:S(2)}) collective-permute-start(bf16[144,128]{1,0:T(8,128)(2,1)S(1)} %get-tuple-element.45.refs_0_), channel_id=1, source_target_pairs={{0,12},{1,4},{2,7},{3,15},{4,1},{5,9},{6,10},{7,2},{8,13},{9,5},{1... | collective-permute-start | bytes 110600 | tf_op jit(solution)/shard_map/ppermute | solution.py:319
  11.5 0.0 collective-permute-start.5
  11.5 1.6 %collective-permute-done.3.refs_1_ = bf16[144,128]{1,0:T(8,128)(2,1)S(1)} collective-permute-done((bf16[144,128]{1,0:T(8,128)(2,1)S(1)}, bf16[144,128]{1,0:T(8,128)(2,1)S(1)}, u32[]{:S(2)}, u32[]{:S(2)}) %collective-permute-start.3) | collective-permute-done | bytes 36896 | tf_op jit(solution)/shard_map/ppermute | solution.py:319
  13.2 1.4 %collective-permute-start.4 = (bf16[144,128]{1,0:T(8,128)(2,1)S(1)}, bf16[144,128]{1,0:T(8,128)(2,1)S(1)}, u32[]{:S(2)}, u32[]{:S(2)}) collective-permute-start(bf16[144,128]{1,0:T(8,128)(2,1)S(1)} %next_sum.3.refs_6_.refs_0_), channel_id=1, source_target_pairs={{0,20},{1,7},{2,4},{3,23},{4,2},{5,17},{6,18},{7,1},{8,14},{9,29},... | collective-permute-start | bytes 110600 | tf_op jit(solution)/shard_map/ppermute | solution.py:319
  14.6 1.1 %backward_mid.1.refs_2_.refs_7_ = f32[9,128,128]{2,1,0:T(8,128)S(1)} custom-call(s32[5,1,8]{2,1,0:T(1,128)S(1)} %bitcast.10, s32[1,8]{1,0:T(1,128)S(1)} %copy-done.7, bf16[1,8,5,128,128]{4,3,2,1,0:T(8,128)(2,1)S(1)} %copy-done.1, bf16[256,128]{1,0:T(8,128)(2,1)S(1)} %copy-done.3, bf16[128,768]{1,0:T(8,128)(2,1)S(1)} %get-tuple-element.30.refs_4_, ...), custom_call_target="tpu_custom_call" | custom-call | flops 1200000000 | bytes 65536 | tf_op jit(solution)/shard_map/backward_mid/pallas_call | solution.py:404
  15.7 0.9 %collective-permute-done.4.refs_1_ = bf16[144,128]{1,0:T(8,128)(2,1)S(1)} collective-permute-done((bf16[144,128]{1,0:T(8,128)(2,1)S(1)}, bf16[144,128]{1,0:T(8,128)(2,1)S(1)}, u32[]{:S(2)}, u32[]{:S(2)}) %collective-permute-start.4) | collective-permute-done | bytes 36896 | tf_op jit(solution)/shard_map/ppermute | solution.py:319
  16.7 1.9 %collective-permute-start.6 = (bf16[144,128]{1,0:T(8,128)(2,1)S(1)}, bf16[144,128]{1,0:T(8,128)(2,1)S(1)}, u32[]{:S(2)}, u32[]{:S(2)}) collective-permute-start(bf16[144,128]{1,0:T(8,128)(2,1)S(1)} %next_sum.4.refs_8_.refs_0_), channel_id=1, source_target_pairs={{0,5},{1,13},{2,14},{3,6},{4,8},{5,0},{6,3},{7,11},{8,4},{9,12},{1... | collective-permute-start | bytes 110600 | tf_op jit(solution)/shard_map/ppermute | solution.py:319
  18.5 1.1 %backward_rim.1.refs_2_.refs_0_ = f32[9,128,128]{2,1,0:T(8,128)S(1)} custom-call(s32[5,1,8]{2,1,0:T(1,128)S(1)} %bitcast.11, s32[1,8]{1,0:T(1,128)S(1)} %copy-done.7, bf16[1,8,5,128,128]{4,3,2,1,0:T(8,128)(2,1)S(1)} %copy-done.1, bf16[256,128]{1,0:T(8,128)(2,1)S(1)} %copy-done.3, bf16[128,768]{1,0:T(8,128)(2,1)S(1)} %get-tuple-element.30.refs_4_, ...), custom_call_target="tpu_custom_call" | custom-call | flops 1200000000 | bytes 65536 | tf_op jit(solution)/shard_map/backward_rim/pallas_call | solution.py:410
  19.6 0.5 %collective-permute-done.6.refs_1_ = bf16[144,128]{1,0:T(8,128)(2,1)S(1)} collective-permute-done((bf16[144,128]{1,0:T(8,128)(2,1)S(1)}, bf16[144,128]{1,0:T(8,128)(2,1)S(1)}, u32[]{:S(2)}, u32[]{:S(2)}) %collective-permute-start.6) | collective-permute-done | bytes 36896 | tf_op jit(solution)/shard_map/ppermute | solution.py:319
  20.2 2.8 %collective-permute-start.7 = (bf16[144,128]{1,0:T(8,128)(2,1)S(1)}, bf16[144,128]{1,0:T(8,128)(2,1)S(1)}, u32[]{:S(2)}, u32[]{:S(2)}) collective-permute-start(bf16[144,128]{1,0:T(8,128)(2,1)S(1)} %next_sum.5.refs_5_.refs_0_), channel_id=1, source_target_pairs={{0,6},{1,21},{2,22},{3,5},{4,16},{5,3},{6,0},{7,19},{8,28},{9,15},... | collective-permute-start | bytes 110600 | tf_op jit(solution)/shard_map/ppermute | solution.py:319
  23.0 0.0 collective-permute-done.5.refs_2_
  23.0 1.0 %gather_outputs.1 = (f32[1,1024,128]{2,1,0:T(8,128)}, bf16[1,1024,128]{2,1,0:T(8,128)(2,1)}, f32[8,128]{1,0:T(8,128)S(1)}) custom-call(f32[9,128,128]{2,1,0:T(8,128)S(1)} %backward_rim.1.refs_2_.refs_0_, bf16[400,128]{1,0:T(8,128)(2,1)S(1)} %collective-permute-done.2.refs_1_, bf16[256,128]{1,0:T(8,128)(2,1)S(1)} %collective-permute-done.5.refs_2_, ...), custom_call_target="tpu_custom_call" | custom-call | flops 1000000000 | bytes 65536 | tf_op jit(solution)/shard_map/gather_outputs/pallas_call | solution.py:416
  24.0 0.6 %collective-permute-done.7.refs_1_ = bf16[144,128]{1,0:T(8,128)(2,1)S(1)} collective-permute-done((bf16[144,128]{1,0:T(8,128)(2,1)S(1)}, bf16[144,128]{1,0:T(8,128)(2,1)S(1)}, u32[]{:S(2)}, u32[]{:S(2)}) %collective-permute-start.7) | collective-permute-done | bytes 36896 | tf_op jit(solution)/shard_map/ppermute | solution.py:319
  24.7 0.3 collective-permute-start.8
  24.9 1.1 %collective-permute-done.8.refs_1_ = f32[136,128]{1,0:T(8,128)S(1)} collective-permute-done((f32[136,128]{1,0:T(8,128)S(1)}, f32[136,128]{1,0:T(8,128)S(1)}, u32[]{:S(2)}, u32[]{:S(2)}) %collective-permute-start.8) | collective-permute-done | bytes 69664 | tf_op jit(solution)/shard_map/ppermute | solution.py:309
  26.0 0.7 %finish.1 = (f32[256,128]{1,0:T(8,128)}, f32[1,128]{1,0:T(1,128)}) custom-call(f32[136,128]{1,0:T(8,128)S(1)} %last_sum.1.refs_0_, f32[136,128]{1,0:T(8,128)S(1)} %collective-permute-done.8.refs_1_), custom_call_target="tpu_custom_call" | custom-call | flops 1000000000 | bytes 65536 | tf_op jit(solution)/shard_map/finish/pallas_call | solution.py:445
  (6 shorter events, 0.2 us)
Async XLA Ops:
  1.5 3.3 %copy-start = (bf16[1,1024,128]{2,1,0:T(8,128)(2,1)S(1)}, bf16[1,1024,128]{2,1,0:T(8,128)(2,1)}, u32[]{:S(2)}) copy-start(bf16[1,1024,128]{2,1,0:T(8,128)(2,1)} %refs_2_.3) | copy-start | bytes 786436
  1.5 3.3 %copy-start.1 = (bf16[1,8,5,128,128]{4,3,2,1,0:T(8,128)(2,1)S(1)}, bf16[1,8,5,128,128]{4,3,2,1,0:T(8,128)(2,1)}, u32[]{:S(2)}) copy-start(bf16[1,8,5,128,128]{4,3,2,1,0:T(8,128)(2,1)} %refs_2_.5) | copy-start | bytes 3932164
  1.5 3.3 %copy-start.2 = (bf16[1,1024,128]{2,1,0:T(8,128)(2,1)S(1)}, bf16[1,1024,128]{2,1,0:T(8,128)(2,1)}, u32[]{:S(2)}) copy-start(bf16[1,1024,128]{2,1,0:T(8,128)(2,1)} %refs_8_.1) | copy-start | bytes 786436
  1.6 3.3 %copy-start.3 = (bf16[256,128]{1,0:T(8,128)(2,1)S(1)}, bf16[256,128]{1,0:T(8,128)(2,1)}, u32[]{:S(2)}) copy-start(bf16[256,128]{1,0:T(8,128)(2,1)} %refs_3_.3) | copy-start | bytes 196612
  1.6 3.3 %copy-start.4 = (s32[1,8,5,128]{3,1,2,0:T(8,128)S(1)}, s32[1,8,5,128]{3,1,2,0:T(8,128)}, u32[]{:S(2)}) copy-start(s32[1,8,5,128]{3,1,2,0:T(8,128)} %param.12) | copy-start | bytes 61444
  1.6 3.3 %copy-start.5 = (s32[1,8,5]{1,0,2:T(1,128)S(1)}, s32[1,8,5]{1,0,2:T(1,128)}, u32[]{:S(2)}) copy-start(s32[1,8,5]{1,0,2:T(1,128)} %param.10) | copy-start | bytes 484
  1.6 3.3 %copy-start.6 = (f32[128]{0:T(128)S(1)}, f32[128]{0:T(128)}, u32[]{:S(2)}) copy-start(f32[128]{0:T(128)} %param.14) | copy-start | bytes 1540
  1.6 3.3 %copy-start.7 = (s32[1,8]{1,0:T(1,128)S(1)}, s32[1,8]{1,0:T(1,128)}, u32[]{:S(2)}) copy-start(s32[1,8]{1,0:T(1,128)} %refs_1_.5) | copy-start | bytes 100
  1.7 3.2 %collective-permute-start = (bf16[256,128]{1,0:T(8,128)(2,1)S(1)}, bf16[256,128]{1,0:T(8,128)(2,1)S(1)}, u32[]{:S(2)}, u32[]{:S(2)}) collective-permute-start(bf16[256,128]{1,0:T(8,128)(2,1)S(1)} %get-tuple-element.29), channel_id=1, source_target_pairs={{0,4},{4,0},{8,12},{12,8},{16,20},{20,16},{24,28},{28,24},{1,5},{5... | collective-permute-start | bytes 196616 | tf_op jit(solution)/shard_map/ppermute | solution.py:309
  2.2 4.9 %collective-permute-start.1 = (bf16[256,128]{1,0:T(8,128)(2,1)S(1)}, bf16[256,128]{1,0:T(8,128)(2,1)S(1)}, u32[]{:S(2)}, u32[]{:S(2)}) collective-permute-start(bf16[256,128]{1,0:T(8,128)(2,1)S(1)} %get-tuple-element.31), channel_id=1, source_target_pairs={{0,1},{1,0},{2,3},{3,2},{4,8},{5,9},{6,10},{7,11},{8,4},{9,5},{10,... | collective-permute-start | bytes 196616 | tf_op jit(solution)/shard_map/ppermute | solution.py:332
  7.6 1.4 %collective-permute-start.2 = (bf16[400,128]{1,0:T(8,128)(2,1)S(1)}, bf16[400,128]{1,0:T(8,128)(2,1)S(1)}, u32[]{:S(2)}, u32[]{:S(2)}) collective-permute-start(bf16[400,128]{1,0:T(8,128)(2,1)S(1)} %get-tuple-element.44), channel_id=1, source_target_pairs={{0,4},{4,0},{8,12},{12,8},{16,20},{20,16},{24,28},{28,24},{1,5},{5... | collective-permute-start | bytes 307208 | tf_op jit(solution)/shard_map/ppermute | solution.py:309
  9.0 4.2 %collective-permute-start.3 = (bf16[144,128]{1,0:T(8,128)(2,1)S(1)}, bf16[144,128]{1,0:T(8,128)(2,1)S(1)}, u32[]{:S(2)}, u32[]{:S(2)}) collective-permute-start(bf16[144,128]{1,0:T(8,128)(2,1)S(1)} %get-tuple-element.45.refs_0_), channel_id=1, source_target_pairs={{0,12},{1,4},{2,7},{3,15},{4,1},{5,9},{6,10},{7,2},{8,13},{9,5},{1... | collective-permute-start | bytes 110600 | tf_op jit(solution)/shard_map/ppermute | solution.py:319
  11.5 11.5 %collective-permute-start.5 = (bf16[256,128]{1,0:T(8,128)(2,1)S(1)}, bf16[256,128]{1,0:T(8,128)(2,1)S(1)}, u32[]{:S(2)}, u32[]{:S(2)}) collective-permute-start(bf16[256,128]{1,0:T(8,128)(2,1)S(1)} %get-tuple-element.46), channel_id=1, source_target_pairs={{0,1},{1,0},{2,3},{3,2},{4,8},{5,9},{6,10},{7,11},{8,4},{9,5},{10,... | collective-permute-start | bytes 196616 | tf_op jit(solution)/shard_map/ppermute | solution.py:332
  13.2 3.4 %collective-permute-start.4 = (bf16[144,128]{1,0:T(8,128)(2,1)S(1)}, bf16[144,128]{1,0:T(8,128)(2,1)S(1)}, u32[]{:S(2)}, u32[]{:S(2)}) collective-permute-start(bf16[144,128]{1,0:T(8,128)(2,1)S(1)} %next_sum.3.refs_6_.refs_0_), channel_id=1, source_target_pairs={{0,20},{1,7},{2,4},{3,23},{4,2},{5,17},{6,18},{7,1},{8,14},{9,29},... | collective-permute-start | bytes 110600 | tf_op jit(solution)/shard_map/ppermute | solution.py:319
  16.7 3.5 %collective-permute-start.6 = (bf16[144,128]{1,0:T(8,128)(2,1)S(1)}, bf16[144,128]{1,0:T(8,128)(2,1)S(1)}, u32[]{:S(2)}, u32[]{:S(2)}) collective-permute-start(bf16[144,128]{1,0:T(8,128)(2,1)S(1)} %next_sum.4.refs_8_.refs_0_), channel_id=1, source_target_pairs={{0,5},{1,13},{2,14},{3,6},{4,8},{5,0},{6,3},{7,11},{8,4},{9,12},{1... | collective-permute-start | bytes 110600 | tf_op jit(solution)/shard_map/ppermute | solution.py:319
  20.2 4.5 %collective-permute-start.7 = (bf16[144,128]{1,0:T(8,128)(2,1)S(1)}, bf16[144,128]{1,0:T(8,128)(2,1)S(1)}, u32[]{:S(2)}, u32[]{:S(2)}) collective-permute-start(bf16[144,128]{1,0:T(8,128)(2,1)S(1)} %next_sum.5.refs_5_.refs_0_), channel_id=1, source_target_pairs={{0,6},{1,21},{2,22},{3,5},{4,16},{5,3},{6,0},{7,19},{8,28},{9,15},... | collective-permute-start | bytes 110600 | tf_op jit(solution)/shard_map/ppermute | solution.py:319
  24.7 1.3 %collective-permute-start.8 = (f32[136,128]{1,0:T(8,128)S(1)}, f32[136,128]{1,0:T(8,128)S(1)}, u32[]{:S(2)}, u32[]{:S(2)}) collective-permute-start(f32[136,128]{1,0:T(8,128)S(1)} %last_sum.1.refs_0_), channel_id=1, source_target_pairs={{0,4},{4,0},{8,12},{12,8},{16,20},{20,16},{24,28},{28,24},{1,5},{5... | collective-permute-start | bytes 208904 | tf_op jit(solution)/shard_map/ppermute | solution.py:309
